TPU v7x, 512 devices: a whole 4x4x16 slice. The times are simulated.
512 devices in a mesh: dp: 32 (over z, core), expert: 16 (over x, y).
Axes of the slice: x: 4, y: 4, z: 16, core: 2. Of those that a mesh axis runs over, the one named last changes fastest.
Arguments:
- tokens: bfloat16 [6144, 2560], P(('dp', 'expert')), may hold values from -6 to 6
- norm_scale_vector: float32 [2560], replicated, may hold values from 0.5 to 1.5
- router: bfloat16 [2560, 16], replicated, may hold values from -0.125 to 0.125
- routes: int32 [6144], P(('dp', 'expert')), may hold values from 0 to 15, as said below
- session_speaker: int32 [6144], P(('dp', 'expert')), may hold values from 0 to 31, as said below
- adapter_slots: int32 [16, 32], P('expert'), may hold values from 0 to 31, each once within a row
- speaker_down_weight: bfloat16 [16, 32, 64, 2560], P('expert', 'dp'), may hold values from -0.125 to 0.125
- speaker_up_weight: bfloat16 [16, 32, 64, 2560], P('expert', 'dp'), may hold values from -0.75 to 0.75
- routed_gate_weight: bfloat16 [16, 2560, 4096], P('expert', None, 'dp'), may hold values from -0.125 to 0.125
- routed_up_weight: bfloat16 [16, 2560, 4096], P('expert', None, 'dp'), may hold values from -0.125 to 0.125
- routed_down_weight: bfloat16 [16, 4096, 2560], P('expert', 'dp'), may hold values from -0.09375 to 0.09375
- common_gate_weight: bfloat16 [2560, 4096], P(None, 'dp'), may hold values from -0.125 to 0.125
- common_up_weight: bfloat16 [2560, 4096], P(None, 'dp'), may hold values from -0.125 to 0.125
- common_down_weight: bfloat16 [4096, 2560], P('dp'), may hold values from -0.09375 to 0.09375
Outputs:
- mixed: bfloat16 [6144, 2560], P(('dp', 'expert'))
Inputs may be any that keep to these rules, and one draw needn't show every extreme that they name: `routes`: among the sessions of one device no expert is named more than 2 times, and some expert exactly 2 times; among the sessions of one index of dp (16 devices) no expert is named more than 13 times, and some expert exactly 13 times. `session_speaker`: the sessions of one device all name different adapters. `adapter_slots`: each row is a permutation.
All inputs are finite; a program needn't handle non-finite values.
Results may differ from a plain program's by a relative error of at most 0.014.
Values may be sent and summed in bfloat16 or wider, within the bound.
A program may use at most 64 MiB of HBM per device.

v0:
```python
import jax
import jax.numpy as jnp
from jax import lax
from jax.sharding import PartitionSpec as P

SLOTS = 2


norm_eps = 1e-05


def swiglu(rows_in, gate_weight, up_weight):
    gate_part = jnp.dot(rows_in, gate_weight, preferred_element_type=jnp.float32)
    up_part = jnp.dot(rows_in, up_weight, preferred_element_type=jnp.float32)
    return (jax.nn.silu(gate_part) * up_part).astype(jnp.bfloat16)


def expert_swiglu(rows_in, gate_weight, up_weight):
    gate_part = jnp.einsum(
        "nkbd,kdf->nkbf", rows_in, gate_weight, preferred_element_type=jnp.float32
    )
    up_part = jnp.einsum("nkbd,kdf->nkbf", rows_in, up_weight, preferred_element_type=jnp.float32)
    return (jax.nn.silu(gate_part) * up_part).astype(jnp.bfloat16)


def body(
    tokens,
    norm_scale_vector,
    router,
    routes,
    session_speaker,
    adapter_slots,
    speaker_down_weight,
    speaker_up_weight,
    routed_gate_weight,
    routed_up_weight,
    routed_down_weight,
    common_gate_weight,
    common_up_weight,
    common_down_weight,
):
    sessions = tokens.shape[0]
    model_width = tokens.shape[1]
    members = lax.axis_size("expert")
    owners = lax.axis_size("dp")
    exp_dev = routed_gate_weight.shape[0]
    experts = router.shape[1]
    bucket = (members * sessions + experts - 1) // experts + 1
    local_rows = exp_dev * bucket
    adapters_local = speaker_down_weight.shape[1]
    stored = owners * adapters_local
    expanded_tokens = tokens.astype(jnp.float32)
    scale_rows = lax.rsqrt(
        jnp.mean(expanded_tokens * expanded_tokens, axis=-1, keepdims=True) + norm_eps
    )
    normed = (expanded_tokens * scale_rows * norm_scale_vector).astype(jnp.bfloat16)
    logits = jnp.dot(normed, router, preferred_element_type=jnp.float32)
    expert_ids = lax.broadcasted_iota(jnp.int32, (sessions, experts), 1)
    gate_probability = jax.nn.sigmoid(
        jnp.sum(jnp.where(routes[:, None] == expert_ids, logits, 0.0), axis=1)
    )
    later_index = lax.broadcasted_iota(jnp.int32, (sessions, sessions), 0)
    earlier_index = lax.broadcasted_iota(jnp.int32, (sessions, sessions), 1)
    same_route = (routes[:, None] == routes[None, :]) & (earlier_index < later_index)
    slot_rank = jnp.sum(same_route.astype(jnp.int32), axis=1)
    slot_index = routes * SLOTS + slot_rank
    placing = (
        lax.broadcasted_iota(jnp.int32, (experts * SLOTS, sessions), 0) == slot_index[None, :]
    ).astype(jnp.bfloat16)
    send_rows = jnp.dot(placing, normed, preferred_element_type=jnp.float32).astype(jnp.bfloat16)
    send_rows = send_rows.reshape(members, exp_dev * SLOTS, model_width)
    send_flags = jnp.sum(placing, axis=1).reshape(members, exp_dev * SLOTS)
    got_rows, got_flags = (
        lax.all_to_all(send_rows, "expert", split_axis=0, concat_axis=0, tiled=True),
        lax.all_to_all(send_flags, "expert", split_axis=0, concat_axis=0, tiled=True),
    )
    arrived = got_rows.reshape(members, exp_dev, SLOTS, model_width)
    arrived_flags = (
        got_flags.astype(jnp.int32)
        .reshape(members, exp_dev, SLOTS)
        .transpose(1, 0, 2)
        .reshape(exp_dev, members * SLOTS)
    )
    before_count = jnp.cumsum(arrived_flags, axis=1) - arrived_flags
    bucket_ids = lax.broadcasted_iota(jnp.int32, (exp_dev, bucket, members * SLOTS), 1)
    packing = ((arrived_flags[:, None, :] == 1) & (before_count[:, None, :] == bucket_ids)).astype(
        jnp.bfloat16
    )
    packing = packing.reshape(exp_dev, bucket, members, SLOTS)
    compact = jnp.einsum(
        "kbms,mksd->kbd", packing, arrived, preferred_element_type=jnp.float32
    ).astype(jnp.bfloat16)
    shared_all = lax.all_gather(normed, "dp", axis=0, tiled=True)
    shared_hidden = swiglu(shared_all, common_gate_weight, common_up_weight)
    hidden_piece = shared_hidden
    common_output = lax.psum_scatter(
        jnp.dot(hidden_piece, common_down_weight, preferred_element_type=jnp.float32).astype(
            jnp.bfloat16
        ),
        "dp",
        scatter_dimension=0,
        tiled=True,
    ).astype(jnp.float32)
    routed_all = lax.all_gather(compact.reshape(local_rows, model_width), "dp", axis=0, tiled=True)
    routed_hidden = expert_swiglu(
        routed_all.reshape(owners, exp_dev, bucket, model_width),
        routed_gate_weight,
        routed_up_weight,
    )
    hidden_piece = routed_hidden
    routed_terms = jnp.einsum(
        "nkbf,kfd->nkbd", hidden_piece, routed_down_weight, preferred_element_type=jnp.float32
    )
    routed_out = lax.psum_scatter(
        routed_terms.reshape(local_rows * lax.axis_size("dp"), model_width).astype(jnp.bfloat16),
        "dp",
        scatter_dimension=0,
        tiled=True,
    )
    routed_back = routed_out.reshape(exp_dev, bucket, model_width)
    returning = jnp.einsum(
        "kbms,kbd->mksd", packing, routed_back, preferred_element_type=jnp.float32
    ).astype(jnp.bfloat16)
    returning = returning.reshape(members, exp_dev * SLOTS, model_width)
    home_rows = lax.all_to_all(
        returning, "expert", split_axis=0, concat_axis=0, tiled=True
    ).reshape(experts * SLOTS, model_width)
    local_dispatched = jnp.dot(placing.T, home_rows, preferred_element_type=jnp.float32)
    adapter_ids = lax.broadcasted_iota(jnp.int32, (sessions, stored), 1)
    owner_of = jnp.sum(
        jnp.where(session_speaker[:, None] == adapter_ids, adapter_slots[0][None, :], 0), axis=1
    )
    outbound_tokens = (
        lax.broadcasted_iota(jnp.int32, (stored, sessions), 0) == owner_of[None, :]
    ).astype(jnp.bfloat16)
    outgoing = jnp.dot(outbound_tokens, normed, preferred_element_type=jnp.float32).astype(
        jnp.bfloat16
    )
    outgoing = outgoing.reshape(owners, adapters_local, model_width)
    received_tokens = lax.all_to_all(outgoing, "dp", split_axis=0, concat_axis=0, tiled=True)
    reduced_hidden = jnp.einsum(
        "fnw,nvw->fnv", received_tokens, speaker_down_weight[0], preferred_element_type=jnp.float32
    ).astype(jnp.bfloat16)
    adapter_delta = jnp.einsum(
        "snu,nut->snt", reduced_hidden, speaker_up_weight[0], preferred_element_type=jnp.float32
    ).astype(jnp.bfloat16)
    gathered_back = lax.all_to_all(
        adapter_delta, "dp", split_axis=0, concat_axis=0, tiled=True
    ).reshape(stored, model_width)
    speaker_rows = jnp.dot(outbound_tokens.T, gathered_back, preferred_element_type=jnp.float32)
    mixed = (
        expanded_tokens
        + common_output
        + gate_probability[:, None] * local_dispatched
        + speaker_rows
    )
    return mixed.astype(jnp.bfloat16)


def solution(mesh):
    in_specs = (
        P(("dp", "expert"), None),
        P(),
        P(),
        P(("dp", "expert")),
        P(("dp", "expert")),
        P("expert", None),
        P("expert", "dp", None, None),
        P("expert", "dp", None, None),
        P("expert", None, "dp"),
        P("expert", None, "dp"),
        P("expert", "dp", None),
        P(None, "dp"),
        P(None, "dp"),
        P("dp", None),
    )
    out_specs = P(("dp", "expert"), None)
    return jax.shard_map(body, mesh=mesh, in_specs=in_specs, out_specs=out_specs, check_vma=False)
```

profile of v0, /device:TPU:1, one launch (start us, length us, event | category | flops | bytes accessed | tf_op | source)
XLA Modules:
  0.0 305.9 jit_solution(10727697806647185235)
XLA Ops:
  7.7 1.6 fusion.84
  11.7 7.6 %all-to-all-start = ((bf16[16,1,2]{2,1,0:T(2,128)(2,1)}), bf16[16,1,2]{2,1,0:T(2,128)(2,1)S(1)}, u32[]{:S(2)}, u32[]{:S(2)}) async-start(bf16[16,1,2]{2,1,0:T(2,128)(2,1)} %all_to_all.24), calls=%async_computation | async-start | bytes 16384 | tf_op jit(solution)/shard_map/all_to_all | solution.py:75
  21.2 4.5 %all-to-all-done = bf16[16,1,2]{2,1,0:T(2,128)(2,1)S(1)} async-done(((bf16[16,1,2]{2,1,0:T(2,128)(2,1)}), bf16[16,1,2]{2,1,0:T(2,128)(2,1)S(1)}, u32[]{:S(2)}, u32[]{:S(2)}) %all-to-all-start) | async-done | bytes 96 | tf_op jit(solution)/shard_map/all_to_all | solution.py:75
  25.7 3.5 %all-to-all-start.1 = ((bf16[16,2,2560]{2,1,0:T(2,128)(2,1)}), bf16[16,2,2560]{2,1,0:T(2,128)(2,1)S(1)}, u32[]{:S(2)}, u32[]{:S(2)}) async-start(bf16[16,2,2560]{2,1,0:T(2,128)(2,1)} %reshape.190), calls=%async_computation.1 | async-start | bytes 327680 | tf_op jit(solution)/shard_map/all_to_all | solution.py:74
  29.8 6.1 %all-to-all-done.1 = bf16[16,2,2560]{2,1,0:T(2,128)(2,1)S(1)} async-done(((bf16[16,2,2560]{2,1,0:T(2,128)(2,1)}), bf16[16,2,2560]{2,1,0:T(2,128)(2,1)S(1)}, u32[]{:S(2)}, u32[]{:S(2)}) %all-to-all-start.1) | async-done | bytes 163872 | tf_op jit(solution)/shard_map/all_to_all | solution.py:74
  40.2 36.4 %all_to_all.30 = bf16[32,2,1280]{2,1,0:T(2,128)(2,1)S(1)} all-to-all(bf16[32,2,1280]{2,1,0:T(2,128)(2,1)S(1)} %reshape.226), channel_id=1, replica_groups=mesh['dp'=32,'expert'=16] {'dp'}, dimensions={0} | all-to-all | bytes 327680 | tf_op jit(solution)/shard_map/all_to_all | solution.py:140
  78.6 5.4 %all-to-all-start.4 = ((bf16[32,2,1280]{2,1,0:T(2,128)(2,1)}), bf16[32,2,1280]{2,1,0:T(2,128)(2,1)S(1)}, u32[]{:S(2)}, u32[]{:S(2)}) async-start(bf16[32,2,1280]{2,1,0:T(2,128)(2,1)} %reshape.228), calls=%async_computation.4 | async-start | bytes 327680 | tf_op jit(solution)/shard_map/all_to_all | solution.py:147
  83.9 9.0 %all-gather.5.cloned.1.call-done = bf16[32,12,2560]{2,1,0:T(8,128)(2,1)} async-done(((bf16[1,12,2560]{2,1,0:T(8,128)(2,1)}), bf16[32,12,2560]{2,1,0:T(8,128)(2,1)}) %all-gather.5.cloned.1.call-update) | async-done | bytes 1966096 | tf_op jit(solution)/shard_map/all_gather | solution.py:93
  92.9 2.7 reshape.206
  95.6 1.8 fusion.86
  97.4 4.8 %convolution_convert_fusion.1 = bf16[384,2560]{1,0:T(8,128)(2,1)} fusion(bf16[128,2560]{1,0:T(8,128)(2,1)} %param.27, bf16[384,2560]{1,0:T(8,128)(2,1)S(1)} %reshape.206, bf16[2560,128]{1,0:T(8,128)(2,1)} %param.26, f32[384,128]{1,0:T(8,128)S(1)} %fusion.86), kind=kOutput, calls=%fused_computation.1 | convolution fusion | flops 504594432 | bytes 5439488 | tf_op jit(solution)/shard_map/dot_general | solution.py:97
  102.2 60.7 %all-gather.7.cloned.1.call-done = bf16[32,13,2560]{2,1,0:T(8,128)(2,1)} async-done(((bf16[1,13,2560]{2,1,0:T(8,128)(2,1)}), bf16[32,13,2560]{2,1,0:T(8,128)(2,1)}) %all-gather.7.cloned.1.call-update) | async-done | bytes 2129936 | tf_op jit(solution)/shard_map/all_gather | solution.py:104
  162.9 4.3 %fusion.12 = f32[32,1,13,128]{3,0,2,1:T(8,128)} fusion(bf16[32,13,2560]{2,1,0:T(8,128)(2,1)} %all-gather.7.cloned.1.call-done, bf16[1,2560,128]{2,1,0:T(8,128)(2,1)} %param.22), kind=kOutput, calls=%fused_computation.18 | convolution fusion | flops 272629760 | bytes 2998272 | tf_op jit(solution)/shard_map/nkbd,kdf->nkbf/dot_general | solution.py:19
  167.1 4.9 %fusion.2 = bf16[32,1,13,2560]{3,0,2,1:T(8,128)(2,1)} fusion(bf16[32,13,2560]{2,1,0:T(8,128)(2,1)S(1)} %copy-done.2, bf16[1,128,2560]{2,1,0:T(8,128)(2,1)S(1)} %copy-done, bf16[1,2560,128]{2,1,0:T(8,128)(2,1)} %param.23, f32[32,1,13,128]{3,0,2,1:T(8,128)} %fusion.12), kind=kOutput, calls=%fused_computation.2 | convolution fusion | flops 546643968 | bytes 5783552 | tf_op jit(solution)/shard_map/nkbf,kfd->nkbd/dot_general | solution.py:111
  172.0 2.8 copy.63
  174.8 2.2 convert_element_type.133
  177.0 57.9 %fusion.85 = (bf16[16,2560]{1,0:T(8,128)(2,1)S(1)}, bf16[16,2560]{1,0:T(8,128)(2,1)S(1)}) fusion(bf16[384,2560]{1,0:T(8,128)(2,1)} %convolution_convert_fusion.1, bf16[416,2560]{1,0:T(8,128)(2,1)} %convert_element_type.133), kind=kCustom, calls=%all-reduce-scatter.2 | all-reduce-scatter fusion | flops 2621441 | bytes 4261888
  234.9 4.2 %collective-permute-start.13 = (bf16[13,2560]{1,0:T(8,128)(2,1)S(1)}, bf16[13,2560]{1,0:T(8,128)(2,1)S(1)}, u32[]{:S(2)}, u32[]{:S(2)}) collective-permute-start(bf16[13,2560]{1,0:T(8,128)(2,1)S(1)} %slice.1), channel_id=1, source_target_pairs={{0,96},{16,112},{32,128},{48,144},{64,160},{80,176},{96,192},{112,... | collective-permute-start | bytes 199688
  239.5 3.2 %collective-permute-start.10 = (bf16[16,2560]{1,0:T(8,128)(2,1)S(1)}, bf16[16,2560]{1,0:T(8,128)(2,1)S(1)}, u32[]{:S(2)}, u32[]{:S(2)}) collective-permute-start(bf16[16,2560]{1,0:T(8,128)(2,1)S(1)} %get-tuple-element.8), channel_id=1, source_target_pairs={{0,48},{16,64},{32,80},{48,96},{64,112},{80,128},{96,144},{112,160... | collective-permute-start | bytes 245768
  242.7 4.2 %collective-permute-start.11 = (bf16[16,2560]{1,0:T(8,128)(2,1)S(1)}, bf16[16,2560]{1,0:T(8,128)(2,1)S(1)}, u32[]{:S(2)}, u32[]{:S(2)}) collective-permute-start(bf16[16,2560]{1,0:T(8,128)(2,1)S(1)} %get-tuple-element.8), channel_id=1, source_target_pairs={{0,64},{16,80},{32,96},{48,112},{64,128},{80,144},{96,160},{112,17... | collective-permute-start | bytes 245768
  246.9 5.6 %collective-permute-start.12 = (bf16[16,2560]{1,0:T(8,128)(2,1)S(1)}, bf16[16,2560]{1,0:T(8,128)(2,1)S(1)}, u32[]{:S(2)}, u32[]{:S(2)}) collective-permute-start(bf16[16,2560]{1,0:T(8,128)(2,1)S(1)} %get-tuple-element.8), channel_id=1, source_target_pairs={{0,80},{16,96},{32,112},{48,128},{64,144},{80,160},{96,176},{112,1... | collective-permute-start | bytes 245768
  252.6 2.2 collective-permute-start.8
  254.8 1.9 collective-permute-start.9
  259.5 2.3 collective-permute-start
  261.8 4.6 %collective-permute-start.1 = (bf16[16,2560]{1,0:T(8,128)(2,1)S(1)}, bf16[16,2560]{1,0:T(8,128)(2,1)S(1)}, u32[]{:S(2)}, u32[]{:S(2)}) collective-permute-start(bf16[16,2560]{1,0:T(8,128)(2,1)S(1)} %get-tuple-element.7), channel_id=1, source_target_pairs={{0,32},{16,48},{32,64},{48,80},{64,96},{80,112},{96,128},{112,144}... | collective-permute-start | bytes 245768
  266.4 2.3 collective-permute-start.2
  268.8 2.1 collective-permute-start.3
  270.9 1.6 collective-permute-start.7
  274.8 6.5 %all-to-all-start.2 = ((bf16[16,2,2560]{2,1,0:T(2,128)(2,1)}), bf16[16,2,2560]{2,1,0:T(2,128)(2,1)S(1)}, u32[]{:S(2)}, u32[]{:S(2)}) async-start(bf16[16,2,2560]{2,1,0:T(2,128)(2,1)} %copy.64), calls=%async_computation.2 | async-start | bytes 327680 | tf_op jit(solution)/shard_map/all_to_all | solution.py:125
  281.4 5.0 %collective-permute-start.4 = (bf16[16,2560]{1,0:T(8,128)(2,1)S(1)}, bf16[16,2560]{1,0:T(8,128)(2,1)S(1)}, u32[]{:S(2)}, u32[]{:S(2)}) collective-permute-start(bf16[16,2560]{1,0:T(8,128)(2,1)S(1)} %get-tuple-element.7), channel_id=1, source_target_pairs={{0,80},{16,96},{32,112},{48,128},{64,144},{80,160},{96,176},{112,1... | collective-permute-start | bytes 245768
  286.4 5.2 %collective-permute-start.5 = (bf16[16,2560]{1,0:T(8,128)(2,1)S(1)}, bf16[16,2560]{1,0:T(8,128)(2,1)S(1)}, u32[]{:S(2)}, u32[]{:S(2)}) collective-permute-start(bf16[16,2560]{1,0:T(8,128)(2,1)S(1)} %get-tuple-element.7), channel_id=1, source_target_pairs={{0,96},{16,112},{32,128},{48,144},{64,160},{80,176},{96,192},{112,... | collective-permute-start | bytes 245768
  291.7 3.3 %collective-permute-start.6 = (bf16[16,2560]{1,0:T(8,128)(2,1)S(1)}, bf16[16,2560]{1,0:T(8,128)(2,1)S(1)}, u32[]{:S(2)}, u32[]{:S(2)}) collective-permute-start(bf16[16,2560]{1,0:T(8,128)(2,1)S(1)} %get-tuple-element.7), channel_id=1, source_target_pairs={{0,112},{16,128},{32,144},{48,160},{64,176},{80,192},{96,208},{112... | collective-permute-start | bytes 245768
  (77 shorter events, 20.3 us)
Async XLA Ops:
  6.5 160.6 %copy-start = (bf16[1,128,2560]{2,1,0:T(8,128)(2,1)S(1)}, bf16[1,128,2560]{2,1,0:T(8,128)(2,1)}, u32[]{:S(2)}) copy-start(bf16[1,128,2560]{2,1,0:T(8,128)(2,1)} %param.24) | copy-start | bytes 1966084
  6.5 70.2 %copy-start.4 = (bf16[1,1,64,2560]{3,2,1,0:T(8,128)(2,1)S(1)}, bf16[1,1,64,2560]{3,2,1,0:T(8,128)(2,1)}, u32[]{:S(2)}) copy-start(bf16[1,1,64,2560]{3,2,1,0:T(8,128)(2,1)} %param.20) | copy-start | bytes 983044
  6.5 70.2 %copy-start.3 = (bf16[1,1,64,2560]{3,2,1,0:T(8,128)(2,1)S(1)}, bf16[1,1,64,2560]{3,2,1,0:T(8,128)(2,1)}, u32[]{:S(2)}) copy-start(bf16[1,1,64,2560]{3,2,1,0:T(8,128)(2,1)} %param.21) | copy-start | bytes 983044
  6.5 86.4 %all-gather.5.cloned.1.call-start = ((), (), s32[]{:S(2)}) async-start(), calls=%async_computation.5 | async-start | bytes 2703360 | tf_op jit(solution)/shard_map/all_gather | solution.py:93
  11.7 14.0 %all-to-all-start = ((bf16[16,1,2]{2,1,0:T(2,128)(2,1)}), bf16[16,1,2]{2,1,0:T(2,128)(2,1)S(1)}, u32[]{:S(2)}, u32[]{:S(2)}) async-start(bf16[16,1,2]{2,1,0:T(2,128)(2,1)} %all_to_all.24), calls=%async_computation | async-start | bytes 16384 | tf_op jit(solution)/shard_map/all_to_all | solution.py:75
  25.7 10.3 %all-to-all-start.1 = ((bf16[16,2,2560]{2,1,0:T(2,128)(2,1)}), bf16[16,2,2560]{2,1,0:T(2,128)(2,1)S(1)}, u32[]{:S(2)}, u32[]{:S(2)}) async-start(bf16[16,2,2560]{2,1,0:T(2,128)(2,1)} %reshape.190), calls=%async_computation.1 | async-start | bytes 327680 | tf_op jit(solution)/shard_map/all_to_all | solution.py:74
  29.2 133.6 %all-gather.7.cloned.1.call-start = ((), (), s32[]{:S(2)}) async-start(), calls=%async_computation.6 | async-start | bytes 2703360 | tf_op jit(solution)/shard_map/all_gather | solution.py:104
  78.6 180.8 %all-to-all-start.4 = ((bf16[32,2,1280]{2,1,0:T(2,128)(2,1)}), bf16[32,2,1280]{2,1,0:T(2,128)(2,1)S(1)}, u32[]{:S(2)}, u32[]{:S(2)}) async-start(bf16[32,2,1280]{2,1,0:T(2,128)(2,1)} %reshape.228), calls=%async_computation.4 | async-start | bytes 327680 | tf_op jit(solution)/shard_map/all_to_all | solution.py:147
  162.9 4.3 %copy-start.2 = (bf16[32,13,2560]{2,1,0:T(8,128)(2,1)S(1)}, bf16[32,13,2560]{2,1,0:T(8,128)(2,1)}, u32[]{:S(2)}) copy-start(bf16[32,13,2560]{2,1,0:T(8,128)(2,1)} %all-gather.7.cloned.1.call-done) | copy-start | bytes 6389764
  177.0 62.1 %copy-start.1 = (bf16[12,2560]{1,0:T(8,128)(2,1)S(1)}, bf16[12,2560]{1,0:T(8,128)(2,1)}, u32[]{:S(2)}) copy-start(bf16[12,2560]{1,0:T(8,128)(2,1)} %param.14) | copy-start | bytes 184324
  177.0 62.1 %copy-start.5 = (f32[2560]{0:T(1024)S(1)}, f32[2560]{0:T(1024)}, u32[]{:S(2)}) copy-start(f32[2560]{0:T(1024)} %param.15) | copy-start | bytes 30724
  177.0 62.1 %copy-start.6 = (bf16[2560,16]{0,1:T(8,128)(2,1)S(1)}, bf16[2560,16]{0,1:T(8,128)(2,1)}, u32[]{:S(2)}) copy-start(bf16[2560,16]{0,1:T(8,128)(2,1)} %param.16) | copy-start | bytes 245764
  177.0 62.2 %copy-start.7 = (s32[12]{0:T(128)S(1)}, s32[12]{0:T(128)}, u32[]{:S(2)}) copy-start(s32[12]{0:T(128)} %param.17) | copy-start | bytes 148
  234.9 19.9 %collective-permute-start.13 = (bf16[13,2560]{1,0:T(8,128)(2,1)S(1)}, bf16[13,2560]{1,0:T(8,128)(2,1)S(1)}, u32[]{:S(2)}, u32[]{:S(2)}) collective-permute-start(bf16[13,2560]{1,0:T(8,128)(2,1)S(1)} %slice.1), channel_id=1, source_target_pairs={{0,96},{16,112},{32,128},{48,144},{64,160},{80,176},{96,192},{112,... | collective-permute-start | bytes 199688
  239.5 20.0 %collective-permute-start.10 = (bf16[16,2560]{1,0:T(8,128)(2,1)S(1)}, bf16[16,2560]{1,0:T(8,128)(2,1)S(1)}, u32[]{:S(2)}, u32[]{:S(2)}) collective-permute-start(bf16[16,2560]{1,0:T(8,128)(2,1)S(1)} %get-tuple-element.8), channel_id=1, source_target_pairs={{0,48},{16,64},{32,80},{48,96},{64,112},{80,128},{96,144},{112,160... | collective-permute-start | bytes 245768
  242.7 19.1 %collective-permute-start.11 = (bf16[16,2560]{1,0:T(8,128)(2,1)S(1)}, bf16[16,2560]{1,0:T(8,128)(2,1)S(1)}, u32[]{:S(2)}, u32[]{:S(2)}) collective-permute-start(bf16[16,2560]{1,0:T(8,128)(2,1)S(1)} %get-tuple-element.8), channel_id=1, source_target_pairs={{0,64},{16,80},{32,96},{48,112},{64,128},{80,144},{96,160},{112,17... | collective-permute-start | bytes 245768
  246.9 19.5 %collective-permute-start.12 = (bf16[16,2560]{1,0:T(8,128)(2,1)S(1)}, bf16[16,2560]{1,0:T(8,128)(2,1)S(1)}, u32[]{:S(2)}, u32[]{:S(2)}) collective-permute-start(bf16[16,2560]{1,0:T(8,128)(2,1)S(1)} %get-tuple-element.8), channel_id=1, source_target_pairs={{0,80},{16,96},{32,112},{48,128},{64,144},{80,160},{96,176},{112,1... | collective-permute-start | bytes 245768
  252.6 16.2 %collective-permute-start.8 = (bf16[16,2560]{1,0:T(8,128)(2,1)S(1)}, bf16[16,2560]{1,0:T(8,128)(2,1)S(1)}, u32[]{:S(2)}, u32[]{:S(2)}) collective-permute-start(bf16[16,2560]{1,0:T(8,128)(2,1)S(1)} %get-tuple-element.8), channel_id=1, source_target_pairs={{0,16},{16,32},{32,48},{48,64},{64,80},{80,96},{96,112},{112,128},... | collective-permute-start | bytes 245768
  254.8 16.1 %collective-permute-start.9 = (bf16[16,2560]{1,0:T(8,128)(2,1)S(1)}, bf16[16,2560]{1,0:T(8,128)(2,1)S(1)}, u32[]{:S(2)}, u32[]{:S(2)}) collective-permute-start(bf16[16,2560]{1,0:T(8,128)(2,1)S(1)} %get-tuple-element.8), channel_id=1, source_target_pairs={{0,32},{16,48},{32,64},{48,80},{64,96},{80,112},{96,128},{112,144}... | collective-permute-start | bytes 245768
  259.5 26.9 %collective-permute-start = (bf16[16,2560]{1,0:T(8,128)(2,1)S(1)}, bf16[16,2560]{1,0:T(8,128)(2,1)S(1)}, u32[]{:S(2)}, u32[]{:S(2)}) collective-permute-start(bf16[16,2560]{1,0:T(8,128)(2,1)S(1)} %get-tuple-element.7), channel_id=1, source_target_pairs={{0,16},{16,32},{32,48},{48,64},{64,80},{80,96},{96,112},{112,128},... | collective-permute-start | bytes 245768
  261.8 29.8 %collective-permute-start.1 = (bf16[16,2560]{1,0:T(8,128)(2,1)S(1)}, bf16[16,2560]{1,0:T(8,128)(2,1)S(1)}, u32[]{:S(2)}, u32[]{:S(2)}) collective-permute-start(bf16[16,2560]{1,0:T(8,128)(2,1)S(1)} %get-tuple-element.7), channel_id=1, source_target_pairs={{0,32},{16,48},{32,64},{48,80},{64,96},{80,112},{96,128},{112,144}... | collective-permute-start | bytes 245768
  266.4 28.8 %collective-permute-start.2 = (bf16[16,2560]{1,0:T(8,128)(2,1)S(1)}, bf16[16,2560]{1,0:T(8,128)(2,1)S(1)}, u32[]{:S(2)}, u32[]{:S(2)}) collective-permute-start(bf16[16,2560]{1,0:T(8,128)(2,1)S(1)} %get-tuple-element.7), channel_id=1, source_target_pairs={{0,48},{16,64},{32,80},{48,96},{64,112},{80,128},{96,144},{112,160... | collective-permute-start | bytes 245768
  268.8 26.4 %collective-permute-start.3 = (bf16[16,2560]{1,0:T(8,128)(2,1)S(1)}, bf16[16,2560]{1,0:T(8,128)(2,1)S(1)}, u32[]{:S(2)}, u32[]{:S(2)}) collective-permute-start(bf16[16,2560]{1,0:T(8,128)(2,1)S(1)} %get-tuple-element.7), channel_id=1, source_target_pairs={{0,64},{16,80},{32,96},{48,112},{64,128},{80,144},{96,160},{112,17... | collective-permute-start | bytes 245768
  270.9 10.5 %collective-permute-start.7 = (bf16[12,2560]{1,0:T(8,128)(2,1)S(1)}, bf16[12,2560]{1,0:T(8,128)(2,1)S(1)}, u32[]{:S(2)}, u32[]{:S(2)}) collective-permute-start(bf16[12,2560]{1,0:T(8,128)(2,1)S(1)} %slice), channel_id=1, source_target_pairs={{0,128},{16,144},{32,160},{48,176},{64,192},{80,208},{96,224},{112... | collective-permute-start | bytes 184328
  274.8 23.2 %all-to-all-start.2 = ((bf16[16,2,2560]{2,1,0:T(2,128)(2,1)}), bf16[16,2,2560]{2,1,0:T(2,128)(2,1)S(1)}, u32[]{:S(2)}, u32[]{:S(2)}) async-start(bf16[16,2,2560]{2,1,0:T(2,128)(2,1)} %copy.64), calls=%async_computation.2 | async-start | bytes 327680 | tf_op jit(solution)/shard_map/all_to_all | solution.py:125
  281.4 13.8 %collective-permute-start.4 = (bf16[16,2560]{1,0:T(8,128)(2,1)S(1)}, bf16[16,2560]{1,0:T(8,128)(2,1)S(1)}, u32[]{:S(2)}, u32[]{:S(2)}) collective-permute-start(bf16[16,2560]{1,0:T(8,128)(2,1)S(1)} %get-tuple-element.7), channel_id=1, source_target_pairs={{0,80},{16,96},{32,112},{48,128},{64,144},{80,160},{96,176},{112,1... | collective-permute-start | bytes 245768
  286.4 8.8 %collective-permute-start.5 = (bf16[16,2560]{1,0:T(8,128)(2,1)S(1)}, bf16[16,2560]{1,0:T(8,128)(2,1)S(1)}, u32[]{:S(2)}, u32[]{:S(2)}) collective-permute-start(bf16[16,2560]{1,0:T(8,128)(2,1)S(1)} %get-tuple-element.7), channel_id=1, source_target_pairs={{0,96},{16,112},{32,128},{48,144},{64,160},{80,176},{96,192},{112,... | collective-permute-start | bytes 245768
  291.7 4.8 %collective-permute-start.6 = (bf16[16,2560]{1,0:T(8,128)(2,1)S(1)}, bf16[16,2560]{1,0:T(8,128)(2,1)S(1)}, u32[]{:S(2)}, u32[]{:S(2)}) collective-permute-start(bf16[16,2560]{1,0:T(8,128)(2,1)S(1)} %get-tuple-element.7), channel_id=1, source_target_pairs={{0,112},{16,128},{32,144},{48,160},{64,176},{80,192},{96,208},{112... | collective-permute-start | bytes 245768
Sparse Core Ops, SparseCore 0:
  9.5 83.4 all-gather.4
  95.1 67.7 all-gather.6
where the time goes:
time: 310 us; the launch traced here: 306 us
  blocking collectives  94.3 us (30%)
  waiting for transfers between devices  81.6 us (26%)
  starting transfers between devices  70.9 us (23%)
  matrix products  21.1 us (7%)
  local copies, waits for them, and re-layouts  16 us (5%)
  between operations  15.2 us (5%)
  other arithmetic  6.84 us (2%)
    all_gather x1, waiting for transfers between devices, body(): lax.all_gather(compact.reshape(local_rows, model_width), 'dp', axis=0, ti...  60.7 us
    unnamed x1, blocking collectives  57.9 us
    unnamed x14, starting transfers between devices  47.8 us
    all_to_all x1, blocking collectives, body(): lax.all_to_all(outgoing, 'dp', split_axis=0, concat_axis=0, tiled=True)  36.4 us
    all_gather x1, waiting for transfers between devices, body(): shared_all = lax.all_gather(normed, 'dp', axis=0, tiled=True)  9.01 us
    unnamed x26, local copies, waits for them, and re-layouts  7.83 us
    all_to_all x1, starting transfers between devices, body(): lax.all_to_all(send_flags, 'expert', split_axis=0, concat_axis=0, tiled=T...  7.58 us
    all_to_all x1, starting transfers between devices, body(): lax.all_to_all(returning, 'expert', split_axis=0, concat_axis=0, tiled=True)  6.53 us
  transfers between devices with their start and end apart: 20, of which 5 were waited for; matrix products, arithmetic and copies ran while one was open for 32% of the time, Pallas kernels for 0%

commit v1 on v0

v1 whole, which is shorter than its diff:
```python
import functools

import jax
import jax.numpy as jnp
from jax import lax
from jax.experimental import pallas as pl
from jax.experimental.pallas import tpu as pltpu
from jax.sharding import PartitionSpec as P

SLOTS = 2
MESH = pl.DeviceIdType.MESH
BF = jnp.bfloat16
F32 = jnp.float32
norm_eps = 1e-05
ROWS = 16
CHUNKS = 2


def moe_kernel(
    planes,
    rows_ref,
    router_ref,
    cg_ref,
    rg_ref,
    cu_ref,
    ru_ref,
    cd_ref,
    rd_ref,
    out_ref,
    gath,
    w1,
    w2,
    hid,
    part,
    first,
    recv,
    own_sem,
    wsend,
    wrecv,
    gsend,
    grecv,
    rsend,
    rrecv,
):
    dp = lax.axis_index("dp")
    col = lax.axis_index("expert")
    z = dp // 2
    core = lax.rem(dp, 2)
    width = rows_ref.shape[1]
    part_width = width // CHUNKS
    half = cg_ref.shape[2]
    up_dev = (lax.rem(z + 1, planes) * 2 + core, col)
    down_dev = (lax.rem(z + planes - 1, planes) * 2 + core, col)
    sibling = (z * 2 + 1 - core, col)

    sources = (cg_ref, rg_ref, cu_ref, ru_ref)
    own = []
    for j in range(4):
        own.append(pltpu.make_async_copy(sources[j].at[0], w1.at[j, :, pl.ds(0, half)], own_sem.at[j]))
    for j, ref in enumerate((cd_ref, rd_ref)):
        own.append(
            pltpu.make_async_copy(ref.at[0], w2.at[pl.ds(2 * j * half, half)], own_sem.at[4 + j])
        )
    for copy in own:
        copy.start()

    barrier = pltpu.get_barrier_semaphore()
    for peer in (up_dev, down_dev, sibling):
        pl.semaphore_signal(barrier, inc=1, device_id=peer, device_id_type=MESH)
    gath[z] = rows_ref[...]
    pl.semaphore_wait(barrier, 3)

    def length(d, ch):
        return planes // 2 if (ch < CHUNKS // 2) == (d == 0) else planes // 2 - 1

    sends = []
    last = {}
    for step in range(planes // 2 + 1):
        for ch in range(CHUNKS):
            for d in range(2):
                if step > 0 and step <= length(d, ch):
                    last[d, ch].wait_recv()
                if step >= length(d, ch):
                    continue
                src = lax.rem(z + (planes - step if d == 0 else step), planes)
                piece = gath.at[src, :, pl.ds(ch * part_width, part_width)]
                copy = pltpu.make_async_remote_copy(
                    piece,
                    piece,
                    gsend.at[d, step, ch],
                    grecv.at[d, step, ch],
                    device_id=up_dev if d == 0 else down_dev,
                    device_id_type=MESH,
                )
                copy.start()
                sends.append(copy)
                last[d, ch] = copy
        if step == 0:
            weights = []
            for j in range(4):
                weights.append((sources[j].at[0], w1.at[j, :, pl.ds(half, half)]))
            for j, ref in enumerate((cd_ref, rd_ref)):
                weights.append((ref.at[0], w2.at[pl.ds((2 * j + 1) * half, half)]))
            shared = []
            for j, (src_ref, dst_ref) in enumerate(weights):
                copy = pltpu.make_async_remote_copy(
                    src_ref,
                    dst_ref,
                    wsend.at[j],
                    wrecv.at[j],
                    device_id=sibling,
                    device_id_type=MESH,
                )
                copy.start()
                shared.append(copy)
    for copy in own:
        copy.wait()
    for copy in shared:
        copy.wait()
    for copy in sends:
        copy.wait_send()

    total = planes * ROWS
    rows = gath[...].reshape(total, width)
    logits = jnp.dot(rows, router_ref[...], preferred_element_type=F32)
    lane = lax.broadcasted_iota(jnp.int32, logits.shape, 1)
    chosen = jnp.sum(jnp.where(lane == col, logits, 0.0), axis=1, keepdims=True)
    gate_prob = 1.0 / (1.0 + jnp.exp(-chosen))
    for n in range(2):
        gate = jnp.dot(rows, w1[n], preferred_element_type=F32)
        up = jnp.dot(rows, w1[2 + n], preferred_element_type=F32)
        value = gate / (1.0 + jnp.exp(-gate)) * up
        if n == 1:
            value = value * gate_prob
        hid[:, pl.ds(2 * n * half, 2 * half)] = value.astype(BF)

    @pl.loop(0, width // 256)
    def _(t):
        cols = pl.ds(pl.multiple_of(t * 256, 256), 256)
        product = jnp.dot(hid[...], w2[:, cols], preferred_element_type=F32)
        part[:, :, cols] = product.reshape(planes, ROWS, 256)

    sends = []
    last = {}
    for step in range(planes // 2 + 1):
        for ch in range(CHUNKS):
            for d in range(2):
                n = length(d, ch)
                if step > n:
                    continue
                cols = pl.ds(ch * part_width, part_width)
                if step > 0:
                    last[d, ch].wait_recv()
                if step == n:
                    continue
                dest = lax.rem(z + (n - step if d == 0 else planes - n + step), planes)
                if step == 0:
                    block = first.at[d, :, cols]
                    block[...] = part[dest, :, cols].astype(BF)
                else:
                    block = recv.at[d, step - 1, :, cols]
                    block[...] = (block[...].astype(F32) + part[dest, :, cols]).astype(BF)
                copy = pltpu.make_async_remote_copy(
                    block,
                    recv.at[d, step, :, cols],
                    rsend.at[d, step, ch],
                    rrecv.at[d, step, ch],
                    device_id=up_dev if d == 0 else down_dev,
                    device_id_type=MESH,
                )
                copy.start()
                sends.append(copy)
                last[d, ch] = copy
    for ch in range(CHUNKS):
        cols = pl.ds(ch * part_width, part_width)
        value = part[z, :, cols]
        for d in range(2):
            value = value + recv[d, length(d, ch) - 1, :, cols].astype(F32)
        out_ref[:, cols] = value.astype(BF)
    for copy in sends:
        copy.wait_send()


def moe_call(rows, router, cg, rg, cu, ru, cd, rd):
    planes = lax.axis_size("dp") // 2
    width = rows.shape[1]
    half = cg.shape[2]
    vmem = pl.BlockSpec(memory_space=pltpu.VMEM)
    hbm = pl.BlockSpec(memory_space=pl.ANY)
    dma = pltpu.SemaphoreType.DMA
    steps = planes // 2
    return pl.pallas_call(
        functools.partial(moe_kernel, planes),
        out_shape=jax.ShapeDtypeStruct((ROWS, width), BF),
        in_specs=[vmem, vmem] + [hbm] * 6,
        out_specs=vmem,
        scratch_shapes=[
            pltpu.VMEM((planes, ROWS, width), BF),
            pltpu.VMEM((4, width, 2 * half), BF),
            pltpu.VMEM((4 * half, width), BF),
            pltpu.VMEM((planes * ROWS, 4 * half), BF),
            pltpu.VMEM((planes, ROWS, width), F32),
            pltpu.VMEM((2, ROWS, width), BF),
            pltpu.VMEM((2, steps, ROWS, width), BF),
            dma((6,)),
            dma((6,)),
            dma((6,)),
            dma((2, steps, CHUNKS)),
            dma((2, steps, CHUNKS)),
            dma((2, steps, CHUNKS)),
            dma((2, steps, CHUNKS)),
        ],
        compiler_params=pltpu.CompilerParams(
            collective_id=1, has_side_effects=True, vmem_limit_bytes=56 * 1024 * 1024
        ),
    )(rows, router, cg, rg, cu, ru, cd, rd)


def body(
    tokens,
    norm_scale_vector,
    router,
    routes,
    session_speaker,
    adapter_slots,
    speaker_down_weight,
    speaker_up_weight,
    routed_gate_weight,
    routed_up_weight,
    routed_down_weight,
    common_gate_weight,
    common_up_weight,
    common_down_weight,
):
    sessions = tokens.shape[0]
    model_width = tokens.shape[1]
    members = lax.axis_size("expert")
    owners = lax.axis_size("dp")
    experts = router.shape[1]
    bucket = ROWS
    expanded_tokens = tokens.astype(jnp.float32)
    scale_rows = lax.rsqrt(
        jnp.mean(expanded_tokens * expanded_tokens, axis=-1, keepdims=True) + norm_eps
    )
    normed = (expanded_tokens * scale_rows * norm_scale_vector).astype(jnp.bfloat16)
    later_index = lax.broadcasted_iota(jnp.int32, (sessions, sessions), 0)
    earlier_index = lax.broadcasted_iota(jnp.int32, (sessions, sessions), 1)
    same_route = (routes[:, None] == routes[None, :]) & (earlier_index < later_index)
    slot_rank = jnp.sum(same_route.astype(jnp.int32), axis=1)
    slot_index = routes * SLOTS + slot_rank
    placing = (
        lax.broadcasted_iota(jnp.int32, (experts * SLOTS, sessions), 0) == slot_index[None, :]
    ).astype(jnp.bfloat16)
    send_rows = jnp.dot(placing, normed, preferred_element_type=jnp.float32).astype(jnp.bfloat16)
    send_rows = send_rows.reshape(members, SLOTS, model_width)
    send_flags = jnp.sum(placing, axis=1).reshape(members, SLOTS)
    got_rows, got_flags = (
        lax.all_to_all(send_rows, "expert", split_axis=0, concat_axis=0, tiled=True),
        lax.all_to_all(send_flags, "expert", split_axis=0, concat_axis=0, tiled=True),
    )
    arrived_flags = got_flags.astype(jnp.int32).reshape(1, members * SLOTS)
    before_count = jnp.cumsum(arrived_flags, axis=1) - arrived_flags
    bucket_ids = lax.broadcasted_iota(jnp.int32, (bucket, members * SLOTS), 0)
    packing = ((arrived_flags == 1) & (before_count == bucket_ids)).astype(jnp.bfloat16)
    compact = jnp.dot(
        packing,
        got_rows.reshape(members * SLOTS, model_width),
        preferred_element_type=jnp.float32,
    ).astype(jnp.bfloat16)
    routed_back = moe_call(
        compact,
        router,
        common_gate_weight[None],
        routed_gate_weight,
        common_up_weight[None],
        routed_up_weight,
        common_down_weight[None],
        routed_down_weight,
    )
    returning = jnp.dot(packing.T, routed_back, preferred_element_type=jnp.float32).astype(
        jnp.bfloat16
    )
    returning = returning.reshape(members, SLOTS, model_width)
    home_rows = lax.all_to_all(
        returning, "expert", split_axis=0, concat_axis=0, tiled=True
    ).reshape(experts * SLOTS, model_width)
    local_dispatched = jnp.dot(placing.T, home_rows, preferred_element_type=jnp.float32)
    adapter_ids = lax.broadcasted_iota(jnp.int32, (sessions, owners), 1)
    owner_of = jnp.sum(
        jnp.where(session_speaker[:, None] == adapter_ids, adapter_slots[0][None, :], 0), axis=1
    )
    outbound_tokens = (
        lax.broadcasted_iota(jnp.int32, (owners, sessions), 0) == owner_of[None, :]
    ).astype(jnp.bfloat16)
    outgoing = jnp.dot(outbound_tokens, normed, preferred_element_type=jnp.float32).astype(
        jnp.bfloat16
    )
    outgoing = outgoing.reshape(owners, 1, model_width)
    received_tokens = lax.all_to_all(outgoing, "dp", split_axis=0, concat_axis=0, tiled=True)
    reduced_hidden = jnp.einsum(
        "fnw,nvw->fnv", received_tokens, speaker_down_weight[0], preferred_element_type=jnp.float32
    ).astype(jnp.bfloat16)
    adapter_delta = jnp.einsum(
        "snu,nut->snt", reduced_hidden, speaker_up_weight[0], preferred_element_type=jnp.float32
    ).astype(jnp.bfloat16)
    gathered_back = lax.all_to_all(
        adapter_delta, "dp", split_axis=0, concat_axis=0, tiled=True
    ).reshape(owners, model_width)
    speaker_rows = jnp.dot(outbound_tokens.T, gathered_back, preferred_element_type=jnp.float32)
    mixed = expanded_tokens + local_dispatched + speaker_rows
    return mixed.astype(jnp.bfloat16)


def solution(mesh):
    in_specs = (
        P(("dp", "expert"), None),
        P(),
        P(),
        P(("dp", "expert")),
        P(("dp", "expert")),
        P("expert", None),
        P("expert", "dp", None, None),
        P("expert", "dp", None, None),
        P("expert", None, "dp"),
        P("expert", None, "dp"),
        P("expert", "dp", None),
        P(None, "dp"),
        P(None, "dp"),
        P("dp", None),
    )
    out_specs = P(("dp", "expert"), None)
    return jax.shard_map(body, mesh=mesh, in_specs=in_specs, out_specs=out_specs, check_vma=False)
```

time: 310 us -> 158 us (0.51); the launches traced: 306 us -> 157 us
  blocking collectives: 94.3 us -> 0 us
  Pallas kernels: 0 us -> 61.8 us
  waiting for transfers between devices: 81.6 us -> 26.5 us
  starting transfers between devices: 70.9 us -> 52.7 us
  matrix products: 21.1 us -> 3.98 us
  between operations: 15.2 us -> 0.2 us
  local copies, waits for them, and re-layouts: 16 us -> 7.88 us
    all_gather x2 -> x0, waiting for transfers between devices: 69.7 us -> none  [the longest x1 60.7 us: body(): lax.all_gather(compact.reshape(local_rows, model_width), 'dp', axis=0, ti...]
    pallas_call x0 -> x1, Pallas kernels: none -> 61.8 us  [moe_call(): pl.pallas_call(functools.partial(moe_kernel, planes), out_shape=jax.Shape...]
    unnamed x1 -> x0, blocking collectives: 57.9 us -> none
    unnamed x14 -> x0, starting transfers between devices: 47.8 us -> none
    all_to_all x1 -> x0, blocking collectives: 36.4 us -> none  [body(): lax.all_to_all(outgoing, 'dp', split_axis=0, concat_axis=0, tiled=True)]
    all_to_all x0 -> x1, starting transfers between devices: none -> 18.5 us  [body(): lax.all_to_all(outgoing, 'dp', split_axis=0, concat_axis=0, tiled=True)]
    all_to_all x1, waiting for transfers between devices: 0.01 us -> 16.9 us  [body(): lax.all_to_all(adapter_delta, 'dp', split_axis=0, concat_axis=0, tiled=True)]
    dot_general x7 -> x2, matrix products: 17.2 us -> 1.91 us  [the longest x1 1.12 us: body(): jnp.dot(packing.T, routed_back, preferred_element_type=jnp.float32)]
  transfers between devices with their start and end apart: 20 -> 5, of which waited for: 5 -> 4; matrix products, arithmetic and copies ran while one was open for 32% -> 7% of each run, Pallas kernels for 0% -> 39%
where the time goes in v1:
time: 158 us; the launch traced here: 157 us
  Pallas kernels  61.8 us (39%)
  starting transfers between devices  52.7 us (33%)
  waiting for transfers between devices  26.5 us (17%)
  local copies, waits for them, and re-layouts  7.88 us (5%)
  matrix products  3.98 us (3%)
  other arithmetic  3.91 us (2%)
    pallas_call x1, Pallas kernels, moe_call(): pl.pallas_call(functools.partial(moe_kernel, planes), out_shape=jax.Shape...  61.8 us
    all_to_all x1, starting transfers between devices, body(): lax.all_to_all(adapter_delta, 'dp', split_axis=0, concat_axis=0, tiled=True)  19.6 us
    all_to_all x1, starting transfers between devices, body(): lax.all_to_all(outgoing, 'dp', split_axis=0, concat_axis=0, tiled=True)  18.5 us
    all_to_all x1, waiting for transfers between devices, body(): lax.all_to_all(adapter_delta, 'dp', split_axis=0, concat_axis=0, tiled=True)  16.9 us
    all_to_all x1, starting transfers between devices, body(): lax.all_to_all(send_flags, 'expert', split_axis=0, concat_axis=0, tiled=T...  7.58 us
    unnamed x21, local copies, waits for them, and re-layouts  4.87 us
    all_to_all x1, waiting for transfers between devices, body(): lax.all_to_all(returning, 'expert', split_axis=0, concat_axis=0, tiled=True)  3.91 us
    all_to_all x1, starting transfers between devices, body(): lax.all_to_all(returning, 'expert', split_axis=0, concat_axis=0, tiled=True)  3.52 us
  transfers between devices with their start and end apart: 5, of which 4 were waited for; matrix products, arithmetic and copies ran while one was open for 7% of the time, Pallas kernels for 39%

profile of v1, /device:TPU:1, one launch (start us, length us, event | category | flops | bytes accessed | tf_op | source)
XLA Modules:
  0.0 157.1 jit_solution(2844348473180770859)
XLA Ops:
  0.0 0.9 convert_reduce_fusion
  1.1 0.7 all_to_all.24
  1.8 7.6 %all-to-all-start = ((bf16[16,1,2]{2,1,0:T(2,128)(2,1)}), bf16[16,1,2]{2,1,0:T(2,128)(2,1)S(1)}, u32[]{:S(2)}, u32[]{:S(2)}) async-start(bf16[16,1,2]{2,1,0:T(2,128)(2,1)} %all_to_all.24), calls=%async_computation | async-start | bytes 16384 | tf_op jit(solution)/shard_map/all_to_all | solution.py:259
  9.4 1.0 fusion.6
  10.4 0.3 convolution_convert_fusion.1
  10.8 0.6 copy-done.6
  11.4 0.2 select_reduce_fusion
  11.6 0.7 reshape.100
  12.3 3.4 %all-to-all-done = bf16[16,1,2]{2,1,0:T(2,128)(2,1)S(1)} async-done(((bf16[16,1,2]{2,1,0:T(2,128)(2,1)}), bf16[16,1,2]{2,1,0:T(2,128)(2,1)S(1)}, u32[]{:S(2)}, u32[]{:S(2)}) %all-to-all-start) | async-done | bytes 96 | tf_op jit(solution)/shard_map/all_to_all | solution.py:259
  15.7 3.5 %all-to-all-start.1 = ((bf16[16,2,2560]{2,1,0:T(2,128)(2,1)}), bf16[16,2,2560]{2,1,0:T(2,128)(2,1)S(1)}, u32[]{:S(2)}, u32[]{:S(2)}) async-start(bf16[16,2,2560]{2,1,0:T(2,128)(2,1)} %reshape.100), calls=%async_computation.1 | async-start | bytes 327680 | tf_op jit(solution)/shard_map/all_to_all | solution.py:258
  19.2 0.2 fusion
  19.5 0.6 copy-done.3
  20.1 1.1 copy.31.router_ref
  21.2 0.6 broadcast.43
  21.8 0.7 reduce.8
  22.5 0.7 reshape.123
  23.6 2.4 %all-to-all-done.1 = bf16[16,2,2560]{2,1,0:T(2,128)(2,1)S(1)} async-done(((bf16[16,2,2560]{2,1,0:T(2,128)(2,1)}), bf16[16,2,2560]{2,1,0:T(2,128)(2,1)S(1)}, u32[]{:S(2)}, u32[]{:S(2)}) %all-to-all-start.1) | async-done | bytes 163872 | tf_op jit(solution)/shard_map/all_to_all | solution.py:258
  26.0 18.5 %all-to-all-start.3 = ((bf16[32,2,1280]{2,1,0:T(2,128)(2,1)}), bf16[32,2,1280]{2,1,0:T(2,128)(2,1)S(1)}, u32[]{:S(2)}, u32[]{:S(2)}) async-start(bf16[32,2,1280]{2,1,0:T(2,128)(2,1)} %reshape.123), calls=%async_computation.3 | async-start | bytes 327680 | tf_op jit(solution)/shard_map/all_to_all | solution.py:299
  44.6 0.8 convolution_convert_fusion.4.rows_ref
  45.3 61.8 %shard_map.136 = bf16[16,2560]{1,0:T(8,128)(2,1)} custom-call(bf16[16,2560]{1,0:T(8,128)(2,1)} %convolution_convert_fusion.4.rows_ref, bf16[2560,16]{1,0:T(8,128)(2,1)} %copy.31.router_ref, bf16[1,2560,128]{2,1,0:T(8,128)(2,1)} %bitcast.30, bf16[1,2560,128]{2,1,0:T(8,128)(2,1)} %rg_ref.1, bf16[1,2560,128]{2,1,0:T(8,128)(2,1)} %bitcast.31, ...), custom_call_target="tpu_custom_call" | custom-call | tf_op jit(solution)/shard_map/pallas_call | solution.py:192
  107.2 1.1 convolution_convert_fusion
  108.3 0.7 reshape.102
  109.0 3.5 %all-to-all-start.2 = ((bf16[16,2,2560]{2,1,0:T(2,128)(2,1)}), bf16[16,2,2560]{2,1,0:T(2,128)(2,1)S(1)}, u32[]{:S(2)}, u32[]{:S(2)}) async-start(bf16[16,2,2560]{2,1,0:T(2,128)(2,1)} %reshape.102), calls=%async_computation.2 | async-start | bytes 327680 | tf_op jit(solution)/shard_map/all_to_all | solution.py:284
  112.7 0.8 copy-done.2
  113.5 0.4 fusion.1
  114.0 0.7 reduce.9
  114.7 0.7 reshape.125
  115.4 3.9 %all-to-all-done.2 = bf16[16,2,2560]{2,1,0:T(2,128)(2,1)S(1)} async-done(((bf16[16,2,2560]{2,1,0:T(2,128)(2,1)}), bf16[16,2,2560]{2,1,0:T(2,128)(2,1)S(1)}, u32[]{:S(2)}, u32[]{:S(2)}) %all-to-all-start.2) | async-done | bytes 163872 | tf_op jit(solution)/shard_map/all_to_all | solution.py:284
  119.3 19.6 %all-to-all-start.4 = ((bf16[32,2,1280]{2,1,0:T(2,128)(2,1)}), bf16[32,2,1280]{2,1,0:T(2,128)(2,1)S(1)}, u32[]{:S(2)}, u32[]{:S(2)}) async-start(bf16[32,2,1280]{2,1,0:T(2,128)(2,1)} %reshape.125), calls=%async_computation.4 | async-start | bytes 327680 | tf_op jit(solution)/shard_map/all_to_all | solution.py:306
  139.0 0.2 convolution_add_fusion.1
  139.3 16.9 %all-to-all-done.4 = bf16[32,2,1280]{2,1,0:T(2,128)(2,1)S(1)} async-done(((bf16[32,2,1280]{2,1,0:T(2,128)(2,1)}), bf16[32,2,1280]{2,1,0:T(2,128)(2,1)S(1)}, u32[]{:S(2)}, u32[]{:S(2)}) %all-to-all-start.4) | async-done | bytes 163872 | tf_op jit(solution)/shard_map/all_to_all | solution.py:306
  156.2 0.9 fusion.2
  (29 shorter events, 0.9 us)
Async XLA Ops:
  0.0 112.7 %copy-start = (bf16[1,1,64,2560]{3,2,1,0:T(8,128)(2,1)S(1)}, bf16[1,1,64,2560]{3,2,1,0:T(8,128)(2,1)}, u32[]{:S(2)}) copy-start(bf16[1,1,64,2560]{3,2,1,0:T(8,128)(2,1)} %param.21) | copy-start | bytes 983044
  0.0 0.9 copy-start.5
  0.0 10.4 %copy-start.1 = (bf16[12,2560]{1,0:T(8,128)(2,1)S(1)}, bf16[12,2560]{1,0:T(8,128)(2,1)}, u32[]{:S(2)}) copy-start(bf16[12,2560]{1,0:T(8,128)(2,1)} %param.14) | copy-start | bytes 184324
  1.8 13.9 %all-to-all-start = ((bf16[16,1,2]{2,1,0:T(2,128)(2,1)}), bf16[16,1,2]{2,1,0:T(2,128)(2,1)S(1)}, u32[]{:S(2)}, u32[]{:S(2)}) async-start(bf16[16,1,2]{2,1,0:T(2,128)(2,1)} %all_to_all.24), calls=%async_computation | async-start | bytes 16384 | tf_op jit(solution)/shard_map/all_to_all | solution.py:259
  9.3 1.1 copy-start.4
  10.7 0.7 copy-start.6
  10.7 0.7 copy-start.7
  15.7 10.3 %all-to-all-start.1 = ((bf16[16,2,2560]{2,1,0:T(2,128)(2,1)}), bf16[16,2,2560]{2,1,0:T(2,128)(2,1)S(1)}, u32[]{:S(2)}, u32[]{:S(2)}) async-start(bf16[16,2,2560]{2,1,0:T(2,128)(2,1)} %reshape.100), calls=%async_computation.1 | async-start | bytes 327680 | tf_op jit(solution)/shard_map/all_to_all | solution.py:258
  19.2 0.9 copy-start.3
  26.0 83.1 %all-to-all-start.3 = ((bf16[32,2,1280]{2,1,0:T(2,128)(2,1)}), bf16[32,2,1280]{2,1,0:T(2,128)(2,1)S(1)}, u32[]{:S(2)}, u32[]{:S(2)}) async-start(bf16[32,2,1280]{2,1,0:T(2,128)(2,1)} %reshape.123), calls=%async_computation.3 | async-start | bytes 327680 | tf_op jit(solution)/shard_map/all_to_all | solution.py:299
  109.0 10.3 %all-to-all-start.2 = ((bf16[16,2,2560]{2,1,0:T(2,128)(2,1)}), bf16[16,2,2560]{2,1,0:T(2,128)(2,1)S(1)}, u32[]{:S(2)}, u32[]{:S(2)}) async-start(bf16[16,2,2560]{2,1,0:T(2,128)(2,1)} %reshape.102), calls=%async_computation.2 | async-start | bytes 327680 | tf_op jit(solution)/shard_map/all_to_all | solution.py:284
  112.6 1.0 copy-start.2
  119.3 36.8 %all-to-all-start.4 = ((bf16[32,2,1280]{2,1,0:T(2,128)(2,1)}), bf16[32,2,1280]{2,1,0:T(2,128)(2,1)S(1)}, u32[]{:S(2)}, u32[]{:S(2)}) async-start(bf16[32,2,1280]{2,1,0:T(2,128)(2,1)} %reshape.125), calls=%async_computation.4 | async-start | bytes 327680 | tf_op jit(solution)/shard_map/all_to_all | solution.py:306

commit v2 on v0

v2 whole, which is shorter than its diff:
```python
import functools

import jax
import jax.numpy as jnp
from jax import lax
from jax.experimental import pallas as pl
from jax.experimental.pallas import tpu as pltpu
from jax.sharding import PartitionSpec as P

MESH = pl.DeviceIdType.MESH
BF = jnp.bfloat16
F32 = jnp.float32
I32 = jnp.int32
norm_eps = 1e-05
ROWS = 16
LANES = 128
PACK = 8


def iota(shape, dim):
    return lax.broadcasted_iota(I32, shape, dim)


def one_hot(condition):
    return jnp.where(condition, 1.0, 0.0).astype(BF)


def stack(rows, fill):
    tiles = rows.shape[1] // LANES
    columns = []
    for t in range(-(-tiles // PACK)):
        pieces = []
        for j in range(PACK):
            i = t * PACK + j
            if i < tiles:
                pieces.append(rows[:, i * LANES : (i + 1) * LANES])
            else:
                pieces.append(jnp.full((ROWS, LANES), fill if i == tiles else 0.0, rows.dtype))
        columns.append(jnp.concatenate(pieces, axis=0))
    return jnp.concatenate(columns, axis=1)


def tile_of(stacked, i):
    t, j = i // PACK, i % PACK
    return stacked[j * ROWS : (j + 1) * ROWS, t * LANES : (t + 1) * LANES]


def unstack(stacked, tiles):
    return jnp.concatenate([tile_of(stacked, i) for i in range(tiles)], axis=1)


def dot(a, b):
    return jnp.dot(a, b, preferred_element_type=F32)


def dot_t(a, b):
    return lax.dot_general(a, b, (((0,), (0,)), ((), ())), preferred_element_type=F32)


def dot_nt(a, b):
    return lax.dot_general(a, b, (((1,), (1,)), ((), ())), preferred_element_type=F32)


def block_kernel(
    planes,
    columns,
    routes_ref,
    speaker_ref,
    slots_ref,
    tokens_ref,
    gain_ref,
    router_ref,
    cg_ref,
    rg_ref,
    cu_ref,
    ru_ref,
    cd_ref,
    rd_ref,
    down_ref,
    up_ref,
    out_ref,
    tok,
    w1,
    w2,
    wd,
    wu,
    xs,
    xr,
    ls,
    lr,
    lr2,
    rs,
    rr,
    bs,
    br,
    br2,
    pack_ref,
    gath,
    hid,
    pb,
    first,
    rb,
    ystage,
    yb,
    own_sem,
    wsem,
    xsem,
    lsem,
    rsem,
    bsem,
    exsem,
    blksem,
    gsem,
    dsem,
    psem,
    qsem,
    ysem,
):
    dp = lax.axis_index("dp")
    col = lax.axis_index("expert")
    z = dp // 2
    core = lax.rem(dp, 2)
    sessions, width = tokens_ref.shape
    tiles = width // LANES
    half = cg_ref.shape[2]
    hops = planes // 2
    side = width // 2
    sibling = (z * 2 + 1 - core, col)

    def plane(offset):
        return lax.rem(z + offset, planes)

    def remote(src, dst, sem, index, device):
        return pltpu.make_async_remote_copy(
            src,
            dst,
            sem.at[(0, *index)],
            sem.at[(1, *index)],
            device_id=device,
            device_id_type=MESH,
        )

    sources = (cg_ref, rg_ref, cu_ref, ru_ref)
    own = []
    for j in range(4):
        own.append(
            pltpu.make_async_copy(sources[j].at[0], w1.at[j, :, pl.ds(0, half)], own_sem.at[j])
        )
    for j, ref in enumerate((cd_ref, rd_ref)):
        own.append(
            pltpu.make_async_copy(ref.at[0], w2.at[pl.ds(2 * j * half, half)], own_sem.at[4 + j])
        )
    own.append(pltpu.make_async_copy(down_ref.at[0, 0], wd, own_sem.at[6]))
    own.append(pltpu.make_async_copy(up_ref.at[0, 0], wu, own_sem.at[7]))
    for copy in own:
        copy.start()

    barrier = pltpu.get_barrier_semaphore()
    pl.semaphore_signal(barrier, inc=1, device_id=sibling, device_id_type=MESH)

    def greet_plane(d, carry):
        pl.semaphore_signal(
            barrier, inc=1, device_id=(plane(d) * 2 + core, col), device_id_type=MESH
        )
        return carry

    def greet_column(d, carry):
        pl.semaphore_signal(
            barrier, inc=1, device_id=(dp, lax.rem(col + d, columns)), device_id_type=MESH
        )
        return carry

    lax.fori_loop(1, planes, greet_plane, 0)
    lax.fori_loop(1, columns, greet_column, 0)

    tok[...] = jnp.zeros_like(tok)
    tok[0:sessions, :] = tokens_ref[...].astype(F32)
    x = tok[...]
    scale = lax.rsqrt(jnp.mean(x * x, axis=-1, keepdims=True) + norm_eps)
    normed = (x * scale * gain_ref[...]).astype(BF)

    routes = [routes_ref[s] for s in range(sessions)]
    route_slot = []
    for s in range(sessions):
        rank = jnp.int32(0)
        for earlier in range(s):
            rank = rank + jnp.where(routes[earlier] == routes[s], 1, 0)
        route_slot.append(routes[s] * 2 + rank)
    storage = [slots_ref[0, speaker_ref[s]] for s in range(sessions)]

    def spread(values, index):
        held = jnp.full(index.shape, -1, I32)
        for s in range(sessions):
            held = jnp.where(index == s, values[s], held)
        return held

    pairs = 2 * PACK
    outer = columns * pairs
    inner = PACK * ROWS
    row = iota((outer, inner), 0)
    lane = iota((outer, inner), 1)
    lane_session = jnp.bitwise_and(iota((1, inner), 1), ROWS - 1)
    same_piece = jnp.bitwise_and(row, PACK - 1) == lane // ROWS
    stacked = stack(normed, 1.0)
    to_expert = one_hot(same_piece & (row // PACK == spread(route_slot, lane_session)))
    xs[...] = dot(to_expert, stacked).astype(BF).reshape(xs.shape)
    to_adapter = one_hot(same_piece & (row // PACK == spread(storage, lane_session)))
    ls[...] = dot(to_adapter, stacked).astype(BF).reshape(ls.shape)

    pl.semaphore_wait(barrier, planes + columns - 1)

    def over_columns(src, dst, sem, d):
        to = lax.rem(col + d, columns)
        return remote(src.at[to], dst.at[col], sem, (d,), (dp, to))

    def over_planes(src, dst, sem, d):
        to = plane(d)
        return remote(src.at[to], dst.at[z], sem, (d,), (to * 2 + core, col))

    def start_all(over, src, dst, sem, count):
        def step(d, carry):
            over(src, dst, sem, d).start()
            return carry

        lax.fori_loop(1, count, step, 0)

    def wait_all(over, src, dst, sem, count):
        def step(d, carry):
            over(src, dst, sem, d).wait()
            return carry

        lax.fori_loop(1, count, step, 0)

    start_all(over_columns, xs, xr, xsem, columns)
    xr[col] = xs[col]
    start_all(over_planes, ls, lr, lsem, planes)
    lr[z] = ls[z]

    shared = []
    for j in range(4):
        shared.append(
            remote(sources[j].at[0], w1.at[j, :, pl.ds(half, half)], wsem, (j,), sibling)
        )
    for j, ref in enumerate((cd_ref, rd_ref)):
        shared.append(
            remote(ref.at[0], w2.at[pl.ds((2 * j + 1) * half, half)], wsem, (4 + j,), sibling)
        )
    for copy in shared:
        copy.start()

    wait_all(over_columns, xs, xr, xsem, columns)
    arrived = xr[...].reshape(outer, 3 * LANES)
    flags = jnp.where(
        jnp.bitwise_and(row, PACK - 1) == tiles % PACK, arrived[:, 2 * LANES :], 0.0
    ).astype(BF)
    left = iota((outer, outer), 0) // PACK
    right = iota((outer, outer), 1) // PACK
    before = dot_t(flags, one_hot(left < right))
    taken = dot_t(flags, one_hot(left == right))
    wide_row = iota((inner, outer), 0)
    wide_lane = iota((inner, outer), 1)
    wide_piece = wide_row // ROWS == jnp.bitwise_and(wide_lane, PACK - 1)
    wide_index = jnp.bitwise_and(wide_row, ROWS - 1)
    pack_ref[...] = one_hot(
        wide_piece & (taken > 0.5) & (jnp.abs(before - wide_index.astype(F32)) < 0.5)
    )
    gath[core, z] = unstack(dot(pack_ref[...], arrived).astype(BF), tiles)

    def pick(half_index):
        return one_hot(
            wide_piece
            & (wide_index == wide_lane // pairs)
            & (jnp.bitwise_and(wide_lane // PACK, 1) == half_index)
        )

    def adapter_meet():
        wait_all(over_planes, ls, lr, lsem, planes)
        remote(lr, lr2, exsem, (0,), sibling).start()

    def adapter_apply():
        remote(lr, lr2, exsem, (0,), sibling).wait()
        for copy in own[6:]:
            copy.wait()
        mine, other = pick(core), pick(1 - core)
        parts = []
        for buffer in (lr, lr2):
            parts.append(unstack(dot(mine, buffer[...].reshape(outer, -1)).astype(BF), tiles))
        low = dot_nt(jnp.concatenate(parts, axis=0), wd[...]).astype(BF)
        delta = dot(low, wu[...]).astype(BF)
        back = dot_t(mine, stack(delta[:ROWS], 0.0)) + dot_t(other, stack(delta[ROWS:], 0.0))
        bs[...] = back.astype(BF).reshape(bs.shape)
        start_all(over_planes, bs, br, bsem, planes)
        br[z] = bs[z]

    def length(d, part):
        return hops if part == d else hops - 1

    near = ((plane(1) * 2 + core, col), (plane(planes - 1) * 2 + core, col))

    def from_plane(d, step):
        return plane(planes - step if d == 0 else step)

    def gather_copy(d, step, h, part):
        piece = gath.at[h, from_plane(d, step), :, pl.ds(part * side, side)]
        return remote(piece, piece, gsem, (d, step, h, part), near[d])

    def hand_over(d, step, part):
        piece = gath.at[0, from_plane(d, step), :, pl.ds(part * side, side)]
        return remote(piece, piece, dsem, (d, step, part), sibling)

    block_copy = remote(gath.at[0, z], gath.at[0, z], blksem, (), sibling)

    @pl.when(core == 1)
    def _():
        for h in (1, 0):
            if h == 0:
                block_copy.wait_recv()
            for part in range(2):
                for d in range(2):
                    gather_copy(d, 0, h, part).start()
        for step in range(1, hops + 1):
            for h in (1, 0):
                for part in range(2):
                    for d in range(2):
                        if step > length(d, part):
                            continue
                        gather_copy(d, step - 1, h, part).wait_recv()
                        if step < length(d, part):
                            gather_copy(d, step, h, part).start()
                        if h == 0:
                            hand_over(d, step, part).start()
            if step == hops - 3:
                adapter_meet()
            if step == hops - 2:
                adapter_apply()
        for step in range(hops):
            for h in (1, 0):
                for part in range(2):
                    for d in range(2):
                        if step < length(d, part):
                            gather_copy(d, step, h, part).wait_send()
                            if h == 0:
                                hand_over(d, step + 1, part).wait_send()

    @pl.when(core == 0)
    def _():
        block_copy.start()
        adapter_meet()
        adapter_apply()
        for step in range(1, hops + 1):
            for part in range(2):
                for d in range(2):
                    if step <= length(d, part):
                        hand_over(d, step, part).wait_recv()
        block_copy.wait_send()

    for copy in own[:6]:
        copy.wait()
    for copy in shared:
        copy.wait()

    rows = gath[core].reshape(planes * ROWS, width)
    logits = dot_nt(rows, router_ref[...])
    chosen = jnp.sum(jnp.where(iota(logits.shape, 1) == col, logits, 0.0), axis=1, keepdims=True)
    gate_prob = 1.0 / (1.0 + jnp.exp(-chosen))
    for n in range(2):
        gate = dot(rows, w1[n])
        value = gate / (1.0 + jnp.exp(-gate)) * dot(rows, w1[2 + n])
        if n == 1:
            value = value * gate_prob
        hid[:, pl.ds(2 * n * half, 2 * half)] = value.astype(BF)

    @pl.loop(0, width // 256)
    def _(t):
        cols = pl.ds(pl.multiple_of(t * 256, 256), 256)
        product = dot(hid[...], w2[:, cols]).astype(BF)
        pb[core, :, :, cols] = product.reshape(planes, ROWS, 256)

    def give(offset):
        dest = plane(offset)
        return remote(pb.at[0, dest], pb.at[0, dest], psem, (offset,), sibling)

    def reduce_copy(d, step, h, part):
        cols = pl.ds(part * side, side)
        src = first.at[d, h, :, cols] if step == 0 else rb.at[d, step - 1, h, :, cols]
        return remote(src, rb.at[d, step, h, :, cols], qsem, (d, step, h, part), near[d])

    order = [hops]
    for distance in range(hops - 1, 0, -1):
        order += [distance, planes - distance]
    order.append(0)
    y_copy = remote(ystage, yb, ysem, (), sibling)

    @pl.when(core == 0)
    def _():
        for offset in order:
            give(offset).start()
        for offset in order:
            give(offset).wait_send()
        y_copy.wait_recv()

    @pl.when(core == 1)
    def _():
        given = set()
        for step in range(hops + 1):
            for h in (1, 0):
                for part in range(2):
                    cols = pl.ds(part * side, side)
                    for d in range(2):
                        n = length(d, part)
                        if step >= n:
                            continue
                        offset = n - step if d == 0 else planes - n + step
                        if h == 0 and offset not in given:
                            give(offset).wait_recv()
                            given.add(offset)
                        dest = plane(offset)
                        if step == 0:
                            first[d, h, :, cols] = pb[h, dest, :, cols]
                        else:
                            reduce_copy(d, step - 1, h, part).wait_recv()
                            rb[d, step - 1, h, :, cols] = (
                                rb[d, step - 1, h, :, cols].astype(F32)
                                + pb[h, dest, :, cols].astype(F32)
                            ).astype(BF)
                        reduce_copy(d, step, h, part).start()
        give(0).wait_recv()
        for h in (0, 1):
            for part in range(2):
                cols = pl.ds(part * side, side)
                value = pb[h, z, :, cols].astype(F32)
                for d in range(2):
                    last = length(d, part) - 1
                    reduce_copy(d, last, h, part).wait_recv()
                    value = value + rb[d, last, h, :, cols].astype(F32)
                if h == 0:
                    ystage[:, cols] = value.astype(BF)
                else:
                    yb[:, cols] = value.astype(BF)
            if h == 0:
                y_copy.start()
        for step in range(hops):
            for h in (1, 0):
                for part in range(2):
                    for d in range(2):
                        if step < length(d, part):
                            reduce_copy(d, step, h, part).wait_send()
        y_copy.wait_send()

    rs[...] = dot_t(pack_ref[...], stack(yb[...], 0.0)).astype(BF).reshape(rs.shape)
    start_all(over_columns, rs, rr, rsem, columns)
    rr[col] = rs[col]

    wait_all(over_planes, bs, br, bsem, planes)
    swap = remote(br, br2, exsem, (1,), sibling)
    swap.start()
    stored = spread(storage, wide_index)
    my_half = jnp.bitwise_and(wide_lane // PACK, 1) == core
    owner = wide_lane // pairs * 2
    swap.wait()
    total = dot(
        one_hot(wide_piece & my_half & (stored == owner + core)), br[...].reshape(outer, -1)
    )
    total += dot(
        one_hot(wide_piece & my_half & (stored == owner + 1 - core)), br2[...].reshape(outer, -1)
    )
    wait_all(over_columns, rs, rr, rsem, columns)
    from_expert = one_hot(wide_piece & (spread(route_slot, wide_index) == wide_lane // PACK))
    total += dot(from_expert, rr[...].reshape(outer, -1))
    for i in range(tiles):
        cols = pl.ds(i * LANES, LANES)
        value = tok[:, cols] + tile_of(total, i)
        out_ref[:, cols] = value[:sessions].astype(BF)


def body(
    tokens,
    norm_scale_vector,
    router,
    routes,
    session_speaker,
    adapter_slots,
    speaker_down_weight,
    speaker_up_weight,
    routed_gate_weight,
    routed_up_weight,
    routed_down_weight,
    common_gate_weight,
    common_up_weight,
    common_down_weight,
):
    sessions, width = tokens.shape
    planes = lax.axis_size("dp") // 2
    columns = lax.axis_size("expert")
    half = common_gate_weight.shape[1]
    rank = speaker_down_weight.shape[2]
    hops = planes // 2
    vmem = pl.BlockSpec(memory_space=pltpu.VMEM)
    smem = pl.BlockSpec(memory_space=pltpu.SMEM)
    hbm = pl.BlockSpec(memory_space=pl.ANY)
    dma = pltpu.SemaphoreType.DMA
    packed = pltpu.VMEM((columns, 2 * PACK, 3 * LANES), BF)
    over_z = pltpu.VMEM((planes, 2 * PACK, 3 * LANES), BF)
    return pl.pallas_call(
        functools.partial(block_kernel, planes, columns),
        out_shape=jax.ShapeDtypeStruct((sessions, width), BF),
        in_specs=[smem] * 3 + [vmem] * 3 + [hbm] * 8,
        out_specs=vmem,
        scratch_shapes=[
            pltpu.VMEM((ROWS, width), F32),
            pltpu.VMEM((4, width, 2 * half), BF),
            pltpu.VMEM((4 * half, width), BF),
            pltpu.VMEM((rank, width), BF),
            pltpu.VMEM((rank, width), BF),
            packed,
            packed,
            over_z,
            over_z,
            over_z,
            packed,
            packed,
            over_z,
            over_z,
            over_z,
            pltpu.VMEM((PACK * ROWS, columns * 2 * PACK), BF),
            pltpu.VMEM((2, planes, ROWS, width), BF),
            pltpu.VMEM((planes * ROWS, 4 * half), BF),
            pltpu.VMEM((2, planes, ROWS, width), BF),
            pltpu.VMEM((2, 2, ROWS, width), BF),
            pltpu.VMEM((2, hops, 2, ROWS, width), BF),
            pltpu.VMEM((ROWS, width), BF),
            pltpu.VMEM((ROWS, width), BF),
            dma((8,)),
            dma((2, 6)),
            dma((2, columns)),
            dma((2, planes)),
            dma((2, columns)),
            dma((2, planes)),
            dma((2, 2)),
            dma((2,)),
            dma((2, 2, hops, 2, 2)),
            dma((2, 2, hops + 1, 2)),
            dma((2, planes)),
            dma((2, 2, hops, 2, 2)),
            dma((2,)),
        ],
        compiler_params=pltpu.CompilerParams(
            collective_id=1, has_side_effects=True, vmem_limit_bytes=56 * 1024 * 1024
        ),
    )(
        routes,
        session_speaker,
        adapter_slots,
        tokens,
        norm_scale_vector[None],
        router.T,
        common_gate_weight[None],
        routed_gate_weight,
        common_up_weight[None],
        routed_up_weight,
        common_down_weight[None],
        routed_down_weight,
        speaker_down_weight,
        speaker_up_weight,
    )


def solution(mesh):
    in_specs = (
        P(("dp", "expert"), None),
        P(),
        P(),
        P(("dp", "expert")),
        P(("dp", "expert")),
        P("expert", None),
        P("expert", "dp", None, None),
        P("expert", "dp", None, None),
        P("expert", None, "dp"),
        P("expert", None, "dp"),
        P("expert", "dp", None),
        P(None, "dp"),
        P(None, "dp"),
        P("dp", None),
    )
    out_specs = P(("dp", "expert"), None)
    return jax.shard_map(body, mesh=mesh, in_specs=in_specs, out_specs=out_specs, check_vma=False)
```

time: 310 us -> 95.9 us (0.31); the launches traced: 306 us -> 95.6 us
  blocking collectives: 94.3 us -> 0 us
  Pallas kernels: 0 us -> 92.8 us
  waiting for transfers between devices: 81.6 us -> 0 us
  starting transfers between devices: 70.9 us -> 0 us
  matrix products: 21.1 us -> 0 us
  between operations: 15.2 us -> 0.01 us
  local copies, waits for them, and re-layouts: 16 us -> 2.84 us
  other arithmetic: 6.84 us -> 0 us
    pallas_call x0 -> x1, Pallas kernels: none -> 92.8 us  [body(): pl.pallas_call(functools.partial(block_kernel, planes, columns), out_shap...]
    all_gather x2 -> x0, waiting for transfers between devices: 69.7 us -> none  [the longest x1 60.7 us: body(): lax.all_gather(compact.reshape(local_rows, model_width), 'dp', axis=0, ti...]
    unnamed x1 -> x0, blocking collectives: 57.9 us -> none
    unnamed x14 -> x0, starting transfers between devices: 47.8 us -> none
    all_to_all x1 -> x0, blocking collectives: 36.4 us -> none  [body(): lax.all_to_all(outgoing, 'dp', split_axis=0, concat_axis=0, tiled=True)]
    all_to_all x4 -> x0, starting transfers between devices: 23 us -> none  [the longest x1 7.58 us: body(): lax.all_to_all(send_flags, 'expert', split_axis=0, concat_axis=0, tiled=T...]
    dot_general x12 -> x0, matrix products: 21.1 us -> none  [the longest x1 4.91 us: body(): jnp.einsum('nkbf,kfd->nkbd', hidden_piece, routed_down_weight, preferred_...]
    all_to_all x4 -> x0, waiting for transfers between devices: 10.6 us -> none  [the longest x1 6.14 us: body(): lax.all_to_all(send_rows, 'expert', split_axis=0, concat_axis=0, tiled=True)]
  transfers between devices with their start and end apart: 20 -> 0, of which waited for: 5 -> 0; matrix products, arithmetic and copies ran while one was open for 32% -> 0% of each run, Pallas kernels for 0% -> 0%
where the time goes in v2:
time: 95.9 us; the launch traced here: 95.6 us
  Pallas kernels  92.8 us (97%)
  local copies, waits for them, and re-layouts  2.84 us (3%)
    pallas_call x1, Pallas kernels, body(): pl.pallas_call(functools.partial(block_kernel, planes, columns), out_shap...  92.8 us

profile of v2, /device:TPU:1, one launch (start us, length us, event | category | flops | bytes accessed | tf_op | source)
XLA Modules:
  0.0 95.6 jit_solution(8632991302110812794)
XLA Ops:
  0.0 1.3 %broadcast_in_dim.12.gain_ref = f32[1,2560]{1,0:T(1,128)} reshape(f32[2560]{0:T(1024)} %param.15) | data formatting | bytes 20480 | tf_op jit(solution)/shard_map/broadcast_in_dim | solution.py:555
  1.3 92.8 %shard_map.136 = bf16[12,2560]{1,0:T(8,128)(2,1)} custom-call(s32[12]{0:T(128)} %routes_ref.1, s32[12]{0:T(128)} %speaker_ref.1, s32[1,32]{1,0:T(1,128)} %slots_ref.1, bf16[12,2560]{1,0:T(8,128)(2,1)} %tokens_ref.1, f32[1,2560]{1,0:T(1,128)} %broadcast_in_dim.12.gain_ref, bf16[16,2560]{1,0:T(8,128)(2,1)} %bitcast.7, bf16[1,2560,128]{2,1,0:T(8,128)(2,1)} %bitcast.4, ...), custom_call_target="tpu_custom_call" | custom-call | tf_op jit(solution)/shard_map/pallas_call | solution.py:504
  94.1 1.5 %copy.16 = bf16[12,2560]{1,0:T(8,128)(2,1)} copy(bf16[12,2560]{1,0:T(8,128)(2,1)} %shard_map.136) | data formatting | bytes 122880

commit v3 on v2

v3 whole, which is shorter than its diff:
```python
import functools

import jax
import jax.numpy as jnp
from jax import lax
from jax.experimental import pallas as pl
from jax.experimental.pallas import tpu as pltpu
from jax.sharding import PartitionSpec as P

MESH = pl.DeviceIdType.MESH
BF = jnp.bfloat16
F32 = jnp.float32
I32 = jnp.int32
norm_eps = 1e-05
ROWS = 16
LANES = 128
PACK = 8


def iota(shape, dim):
    return lax.broadcasted_iota(I32, shape, dim)


def one_hot(condition):
    return jnp.where(condition, 1.0, 0.0).astype(BF)


def stack(rows, fill):
    tiles = rows.shape[1] // LANES
    columns = []
    for t in range(-(-tiles // PACK)):
        pieces = []
        for j in range(PACK):
            i = t * PACK + j
            if i < tiles:
                pieces.append(rows[:, i * LANES : (i + 1) * LANES])
            else:
                pieces.append(jnp.full((ROWS, LANES), fill if i == tiles else 0.0, rows.dtype))
        columns.append(jnp.concatenate(pieces, axis=0))
    return jnp.concatenate(columns, axis=1)


def tile_of(stacked, i):
    t, j = i // PACK, i % PACK
    return stacked[j * ROWS : (j + 1) * ROWS, t * LANES : (t + 1) * LANES]


def unstack(stacked, tiles):
    return jnp.concatenate([tile_of(stacked, i) for i in range(tiles)], axis=1)


def dot(a, b):
    return jnp.dot(a, b, preferred_element_type=F32)


def dot_t(a, b):
    return lax.dot_general(a, b, (((0,), (0,)), ((), ())), preferred_element_type=F32)


def dot_nt(a, b):
    return lax.dot_general(a, b, (((1,), (1,)), ((), ())), preferred_element_type=F32)


def block_kernel(
    planes,
    columns,
    routes_ref,
    speaker_ref,
    slots_ref,
    tokens_ref,
    gain_ref,
    router_ref,
    cg_ref,
    rg_ref,
    cu_ref,
    ru_ref,
    cd_ref,
    rd_ref,
    down_ref,
    up_ref,
    out_ref,
    tok,
    w1,
    w2,
    wd,
    wu,
    xs,
    xr,
    ls,
    ls2,
    ls4,
    lr,
    rs,
    rr,
    bs,
    br,
    pack_ref,
    gath,
    hid,
    pb,
    first,
    rb,
    ystage,
    yb,
    own_sem,
    wsem,
    xsem,
    lsem,
    rsem,
    bsem,
    exsem,
    blksem,
    gsem,
    dsem,
    psem,
    qsem,
    ysem,
):
    dp = lax.axis_index("dp")
    col = lax.axis_index("expert")
    z = dp // 2
    core = lax.rem(dp, 2)
    sessions, width = tokens_ref.shape
    tiles = width // LANES
    half = cg_ref.shape[2]
    hops = planes // 2
    side = width // 2
    sibling = (z * 2 + 1 - core, col)

    def plane(offset):
        return lax.rem(z + offset, planes)

    def remote(src, dst, sem, index, device):
        return pltpu.make_async_remote_copy(
            src,
            dst,
            sem.at[(0, *index)],
            sem.at[(1, *index)],
            device_id=device,
            device_id_type=MESH,
        )

    barrier = pltpu.get_barrier_semaphore()

    def greet(device):
        pl.semaphore_signal(barrier, inc=1, device_id=device, device_id_type=MESH)

    near = ((plane(1) * 2 + core, col), (plane(planes - 1) * 2 + core, col))
    greet(sibling)
    for d in range(1, columns):
        greet((dp, lax.rem(col + d, columns)))

    @pl.when(core == 1)
    def _():
        for device in near:
            greet(device)

    @pl.when(core == 0)
    def _():
        for d in range(1, planes):
            greet((plane(d) * 2, col))

    sources = (cg_ref, rg_ref, cu_ref, ru_ref)
    own = []
    for j in range(4):
        own.append(
            pltpu.make_async_copy(sources[j].at[0], w1.at[j, :, pl.ds(0, half)], own_sem.at[j])
        )
    for j, ref in enumerate((cd_ref, rd_ref)):
        own.append(
            pltpu.make_async_copy(ref.at[0], w2.at[pl.ds(2 * j * half, half)], own_sem.at[4 + j])
        )
    for copy in own:
        copy.start()
    adapter = (
        pltpu.make_async_copy(down_ref.at[0, 0], wd.at[0], own_sem.at[6]),
        pltpu.make_async_copy(up_ref.at[0, 0], wu.at[0], own_sem.at[7]),
    )

    @pl.when(core == 0)
    def _():
        for copy in adapter:
            copy.start()

    tok[...] = jnp.zeros_like(tok)
    tok[0:sessions, :] = tokens_ref[...].astype(F32)
    x = tok[...]
    scale = lax.rsqrt(jnp.mean(x * x, axis=-1, keepdims=True) + norm_eps)
    normed = (x * scale * gain_ref[...][None, :]).astype(BF)

    routes = [routes_ref[s] for s in range(sessions)]
    route_slot = []
    for s in range(sessions):
        rank = jnp.int32(0)
        for earlier in range(s):
            rank = rank + jnp.where(routes[earlier] == routes[s], 1, 0)
        route_slot.append(routes[s] * 2 + rank)
    storage = [slots_ref[0, speaker_ref[s]] for s in range(sessions)]

    def spread(values, index):
        held = jnp.full(index.shape, -1, I32)
        for s in range(sessions):
            held = jnp.where(index == s, values[s], held)
        return held

    pairs = 2 * PACK
    outer = columns * pairs
    inner = PACK * ROWS
    row = iota((outer, inner), 0)
    lane = iota((outer, inner), 1)
    lane_session = jnp.bitwise_and(iota((1, inner), 1), ROWS - 1)
    same_piece = jnp.bitwise_and(row, PACK - 1) == lane // ROWS
    stacked = stack(normed, 1.0)
    to_expert = one_hot(same_piece & (row // PACK == spread(route_slot, lane_session)))
    xs[...] = dot(to_expert, stacked).astype(BF).reshape(xs.shape)
    to_adapter = one_hot(same_piece & (row // PACK == spread(storage, lane_session)))
    tail = stacked[: inner // 2, 2 * LANES :]
    tail = jnp.concatenate([tail, tail], axis=0)
    tail = jnp.where(iota(tail.shape, 0) // (inner // 2) == core, tail.astype(F32), 0.0).astype(BF)
    stacked = jnp.concatenate([stacked[:, : 2 * LANES], tail], axis=1)
    ls[...] = dot(to_adapter, stacked).astype(BF).reshape(ls.shape)

    def over_columns(src, dst, sem, d):
        to = lax.rem(col + d, columns)
        return remote(src.at[to], dst.at[col], sem, (d,), (dp, to))

    def over_planes(src, dst, sem, d):
        to = plane(d)
        return remote(src.at[to], dst.at[z], sem, (d,), (to * 2 + core, col))

    def start_all(over, src, dst, sem, count):
        for d in range(1, count):
            over(src, dst, sem, d).start()

    def wait_all(over, src, dst, sem, count):
        for d in range(1, count):
            over(src, dst, sem, d).wait()

    slots_copy = remote(ls, ls2, exsem, (0,), sibling)
    adapter_copies = (
        remote(down_ref.at[0, 0], wd.at[1], wsem, (6,), sibling),
        remote(up_ref.at[0, 0], wu.at[1], wsem, (7,), sibling),
    )

    @pl.when(core == 1)
    def _():
        pl.semaphore_wait(barrier, columns + 2)
        slots_copy.start()

    @pl.when(core == 0)
    def _():
        pl.semaphore_wait(barrier, columns + planes - 1)

    start_all(over_columns, xs, xr, xsem, columns)
    xr[col] = xs[col]

    @pl.when(core == 0)
    def _():
        slots_copy.wait_recv()
        ls4[:, :, 0 : 2 * LANES] = ls[:, :, 0 : 2 * LANES]
        ls4[:, :, 2 * LANES : 4 * LANES] = ls2[:, :, 0 : 2 * LANES]
        ls4[:, :, 4 * LANES :] = ls[:, :, 2 * LANES :] + ls2[:, :, 2 * LANES :]
        start_all(over_planes, ls4, lr, lsem, planes)
        lr[z] = ls4[z]

    shared = []
    for j in range(4):
        shared.append(
            remote(sources[j].at[0], w1.at[j, :, pl.ds(half, half)], wsem, (j,), sibling)
        )
    for j, ref in enumerate((cd_ref, rd_ref)):
        shared.append(
            remote(ref.at[0], w2.at[pl.ds((2 * j + 1) * half, half)], wsem, (4 + j,), sibling)
        )
    for copy in shared:
        copy.start()

    @pl.when(core == 1)
    def _():
        for copy in adapter_copies:
            copy.start()

    wait_all(over_columns, xs, xr, xsem, columns)
    arrived = xr[...].reshape(outer, 3 * LANES)
    flags = jnp.where(
        jnp.bitwise_and(row, PACK - 1) == tiles % PACK, arrived[:, 2 * LANES :], 0.0
    ).astype(BF)
    left = iota((outer, outer), 0) // PACK
    right = iota((outer, outer), 1) // PACK
    before = dot_t(flags, one_hot(left < right))
    taken = dot_t(flags, one_hot(left == right))
    wide_row = iota((inner, outer), 0)
    wide_lane = iota((inner, outer), 1)
    wide_piece = wide_row // ROWS == jnp.bitwise_and(wide_lane, PACK - 1)
    wide_index = jnp.bitwise_and(wide_row, ROWS - 1)
    pack_ref[...] = one_hot(
        wide_piece & (taken > 0.5) & (jnp.abs(before - wide_index.astype(F32)) < 0.5)
    )
    mine = pl.ds(pl.multiple_of(core * ROWS, ROWS), ROWS)
    gath[z, mine, :] = unstack(dot(pack_ref[...], arrived).astype(BF), tiles)

    def pick(half_index):
        return one_hot(
            wide_piece
            & (wide_index == wide_lane // pairs)
            & (jnp.bitwise_and(wide_lane // PACK, 1) == half_index)
        )

    def adapter_apply():
        wait_all(over_planes, ls4, lr, lsem, planes)
        for copy in adapter:
            copy.wait()
        for copy in adapter_copies:
            copy.wait_recv()
        back = jnp.zeros((outer, 5 * LANES), F32)
        for r in range(2):
            chosen = pick(r)
            got = dot(chosen, lr[...].reshape(outer, 5 * LANES)).astype(BF)
            parts = []
            for source in range(2):
                pieces = []
                for i in range(tiles):
                    t, j = i // PACK, i % PACK
                    if t == 2:
                        t, j = 4, j + 4 * source
                    else:
                        t = t + 2 * source
                    pieces.append(got[j * ROWS : (j + 1) * ROWS, t * LANES : (t + 1) * LANES])
                parts.append(jnp.concatenate(pieces, axis=1))
            low = dot_nt(jnp.concatenate(parts, axis=0), wd[r]).astype(BF)
            delta = dot(low, wu[r]).astype(BF)
            first_stack, second_stack = stack(delta[:ROWS], 0.0), stack(delta[ROWS:], 0.0)
            both = jnp.concatenate(
                [first_stack[: inner // 2, 2 * LANES :], second_stack[: inner // 2, 2 * LANES :]],
                axis=0,
            )
            back += dot_t(
                chosen,
                jnp.concatenate(
                    [first_stack[:, : 2 * LANES], second_stack[:, : 2 * LANES], both], axis=1
                ),
            )
        bs[...] = back.astype(BF).reshape(bs.shape)
        start_all(over_planes, bs, br, bsem, planes)
        br[z] = bs[z]

    def length(d, part):
        return hops if part == d else hops - 1

    def from_plane(d, step):
        return plane(planes - step if d == 0 else step)

    def gather_copy(d, step, h, part):
        piece = gath.at[from_plane(d, step), pl.ds(h * ROWS, ROWS), pl.ds(part * side, side)]
        return remote(piece, piece, gsem, (d, step, h, part), near[d])

    def hand_over(d, step):
        piece = gath.at[from_plane(d, step)]
        return remote(piece, piece, dsem, (d, step), sibling)

    block_copy = remote(gath.at[z, mine, :], gath.at[z, mine, :], blksem, (), sibling)

    reach = hops - 2
    middle = reach // 2
    inner_planes = [0]
    outer_planes = []
    for distance in range(1, reach + 1):
        both = [distance, planes - distance]
        if distance <= middle:
            inner_planes += both
        else:
            outer_planes = both + outer_planes
    given_planes = outer_planes + inner_planes[:0:-1] + [0]

    def weights_here():
        for copy in own:
            copy.wait()
        for copy in shared:
            copy.wait()

    def apply_experts(offsets):
        rows = jnp.concatenate([gath[plane(o)] for o in offsets], axis=0)
        logits = dot_nt(rows, router_ref[...])
        chosen = jnp.where(iota(logits.shape, 1) == col, logits, 0.0)
        gate_prob = 1.0 / (1.0 + jnp.exp(-jnp.sum(chosen, axis=1, keepdims=True)))
        held = pl.ds(0, len(offsets) * 2 * ROWS)
        for n in range(2):
            gate = dot(rows, w1[n])
            value = gate / (1.0 + jnp.exp(-gate)) * dot(rows, w1[2 + n])
            if n == 1:
                value = value * gate_prob
            hid[held, pl.ds(2 * n * half, 2 * half)] = value.astype(BF)

        @pl.loop(0, width // 256)
        def _(t):
            cols = pl.ds(pl.multiple_of(t * 256, 256), 256)
            product = dot(hid[held, :], w2[:, cols]).astype(BF)
            for i, o in enumerate(offsets):
                pb[plane(o), :, cols] = product[i * 2 * ROWS : (i + 1) * 2 * ROWS]

    def give(offset):
        dest = plane(offset)
        return remote(pb.at[dest], pb.at[dest], psem, (offset,), sibling)

    def reduce_copy(d, step, h, part):
        place = (pl.ds(h * ROWS, ROWS), pl.ds(part * side, side))
        src = first.at[(d, *place)] if step == 0 else rb.at[(d, step - 1, *place)]
        return remote(src, rb.at[(d, step, *place)], qsem, (d, step, h, part), near[d])

    def reduce_step(step, chain, given):
        for h in (1, 0):
            for d in range(2):
                part = d if chain == hops else 1 - d
                place = (pl.ds(h * ROWS, ROWS), pl.ds(part * side, side))
                offset = chain - step if d == 0 else planes - chain + step
                if offset in given_planes and offset not in given:
                    give(offset).wait_recv()
                    given.add(offset)
                dest = plane(offset)
                if step == 0:
                    first[(d, *place)] = pb[(dest, *place)]
                else:
                    reduce_copy(d, step - 1, h, part).wait_recv()
                    rb[(d, step - 1, *place)] = (
                        rb[(d, step - 1, *place)].astype(F32) + pb[(dest, *place)].astype(F32)
                    ).astype(BF)
                reduce_copy(d, step, h, part).start()

    @pl.when(core == 1)
    def _():
        block_copy.start()
        for h in (1, 0):
            if h == 0:
                block_copy.wait_recv()
            for part in range(2):
                for d in range(2):
                    gather_copy(d, 0, h, part).start()
        for step in range(1, hops + 1):
            if step == hops:
                weights_here()
                apply_experts([hops - 1, planes - hops + 1])
                reduce_step(0, hops - 1, set())
            for h in (1, 0):
                for part in range(2):
                    for d in range(2):
                        if step > length(d, part):
                            continue
                        gather_copy(d, step - 1, h, part).wait_recv()
                        if step < length(d, part):
                            gather_copy(d, step, h, part).start()
            if step <= reach:
                for d in range(2):
                    hand_over(d, step).start()
        apply_experts([hops])
        reduce_step(0, hops, set())

    @pl.when(core == 0)
    def _():
        block_copy.start()
        weights_here()
        block_copy.wait_recv()
        for step in range(1, reach + 1):
            for d in range(2):
                hand_over(d, step).wait_recv()
            if step == middle:
                apply_experts(inner_planes)
        apply_experts(outer_planes)
        for offset in given_planes:
            give(offset).start()
        adapter_apply()

    y_copy = remote(ystage, yb, ysem, (), sibling)
    delta_copy = remote(br, br, exsem, (1,), sibling)

    @pl.when(core == 0)
    def _():
        wait_all(over_planes, bs, br, bsem, planes)
        delta_copy.start()
        block_copy.wait_send()
        for offset in given_planes:
            give(offset).wait_send()
        delta_copy.wait_send()
        y_copy.wait_recv()

    @pl.when(core == 1)
    def _():
        given = set()
        for step in range(1, hops):
            for chain in (hops - 1, hops):
                if step < chain:
                    reduce_step(step, chain, given)
        give(0).wait_recv()
        for h in (0, 1):
            for part in range(2):
                cols = pl.ds(part * side, side)
                rows = pl.ds(h * ROWS, ROWS)
                value = pb[z, rows, cols].astype(F32)
                for d in range(2):
                    last = length(d, part) - 1
                    reduce_copy(d, last, h, part).wait_recv()
                    value = value + rb[d, last, rows, cols].astype(F32)
                if h == 0:
                    ystage[:, cols] = value.astype(BF)
                else:
                    yb[:, cols] = value.astype(BF)
            if h == 0:
                y_copy.start()

    rs[...] = dot_t(pack_ref[...], stack(yb[...], 0.0)).astype(BF).reshape(rs.shape)
    start_all(over_columns, rs, rr, rsem, columns)
    rr[col] = rs[col]

    @pl.when(core == 1)
    def _():
        slots_copy.wait_send()
        for copy in adapter_copies:
            copy.wait_send()
        for step in range(hops):
            for h in (1, 0):
                for part in range(2):
                    for d in range(2):
                        if step < length(d, part):
                            gather_copy(d, step, h, part).wait_send()
                            reduce_copy(d, step, h, part).wait_send()
        for step in range(1, reach + 1):
            for d in range(2):
                hand_over(d, step).wait_send()
        block_copy.wait_send()
        y_copy.wait_send()
        delta_copy.wait_recv()

    stored = spread(storage, wide_index) == wide_lane // PACK
    body_part = br[:, :, pl.ds(pl.multiple_of(core * 2 * LANES, 2 * LANES), 2 * LANES)]
    tail_part = br[:, :, 4 * LANES :].reshape(outer, LANES)
    tail_piece = wide_row // ROWS + 4 * core == jnp.bitwise_and(wide_lane, PACK - 1)
    total = jnp.concatenate(
        [
            dot(one_hot(wide_piece & stored), body_part.reshape(outer, 2 * LANES)),
            dot(one_hot(tail_piece & stored), tail_part),
        ],
        axis=1,
    )
    wait_all(over_columns, rs, rr, rsem, columns)
    from_expert = one_hot(wide_piece & (spread(route_slot, wide_index) == wide_lane // PACK))
    total += dot(from_expert, rr[...].reshape(outer, -1))
    for i in range(tiles):
        cols = pl.ds(i * LANES, LANES)
        value = tok[:, cols] + tile_of(total, i)
        out_ref[:, cols] = value[:sessions].astype(BF)


def body(
    tokens,
    norm_scale_vector,
    router,
    routes,
    session_speaker,
    adapter_slots,
    speaker_down_weight,
    speaker_up_weight,
    routed_gate_weight,
    routed_up_weight,
    routed_down_weight,
    common_gate_weight,
    common_up_weight,
    common_down_weight,
):
    sessions, width = tokens.shape
    planes = lax.axis_size("dp") // 2
    columns = lax.axis_size("expert")
    half = common_gate_weight.shape[1]
    rank = speaker_down_weight.shape[2]
    hops = planes // 2
    vmem = pl.BlockSpec(memory_space=pltpu.VMEM)
    smem = pl.BlockSpec(memory_space=pltpu.SMEM)
    hbm = pl.BlockSpec(memory_space=pl.ANY)
    dma = pltpu.SemaphoreType.DMA
    packed = pltpu.VMEM((columns, 2 * PACK, 3 * LANES), BF)
    over_z = pltpu.VMEM((planes, 2 * PACK, 3 * LANES), BF)
    wide_z = pltpu.VMEM((planes, 2 * PACK, 5 * LANES), BF)
    return pl.pallas_call(
        functools.partial(block_kernel, planes, columns),
        out_shape=jax.ShapeDtypeStruct((sessions, width), BF),
        in_specs=[smem] * 3 + [vmem] * 3 + [hbm] * 8,
        out_specs=vmem,
        scratch_shapes=[
            pltpu.VMEM((ROWS, width), F32),
            pltpu.VMEM((4, width, 2 * half), BF),
            pltpu.VMEM((4 * half, width), BF),
            pltpu.VMEM((2, rank, width), BF),
            pltpu.VMEM((2, rank, width), BF),
            packed,
            packed,
            over_z,
            over_z,
            wide_z,
            wide_z,
            packed,
            packed,
            wide_z,
            wide_z,
            pltpu.VMEM((PACK * ROWS, columns * 2 * PACK), BF),
            pltpu.VMEM((planes, 2 * ROWS, width), BF),
            pltpu.VMEM((planes * ROWS, 4 * half), BF),
            pltpu.VMEM((planes, 2 * ROWS, width), BF),
            pltpu.VMEM((2, 2 * ROWS, width), BF),
            pltpu.VMEM((2, hops, 2 * ROWS, width), BF),
            pltpu.VMEM((ROWS, width), BF),
            pltpu.VMEM((ROWS, width), BF),
            dma((8,)),
            dma((2, 8)),
            dma((2, columns)),
            dma((2, planes)),
            dma((2, columns)),
            dma((2, planes)),
            dma((2, 2)),
            dma((2,)),
            dma((2, 2, hops, 2, 2)),
            dma((2, 2, hops)),
            dma((2, planes)),
            dma((2, 2, hops, 2, 2)),
            dma((2,)),
        ],
        compiler_params=pltpu.CompilerParams(
            collective_id=1, has_side_effects=True, vmem_limit_bytes=56 * 1024 * 1024
        ),
    )(
        routes,
        session_speaker,
        adapter_slots,
        tokens,
        norm_scale_vector,
        router.T,
        common_gate_weight[None],
        routed_gate_weight,
        common_up_weight[None],
        routed_up_weight,
        common_down_weight[None],
        routed_down_weight,
        speaker_down_weight,
        speaker_up_weight,
    )


def solution(mesh):
    in_specs = (
        P(("dp", "expert"), None),
        P(),
        P(),
        P(("dp", "expert")),
        P(("dp", "expert")),
        P("expert", None),
        P("expert", "dp", None, None),
        P("expert", "dp", None, None),
        P("expert", None, "dp"),
        P("expert", None, "dp"),
        P("expert", "dp", None),
        P(None, "dp"),
        P(None, "dp"),
        P("dp", None),
    )
    out_specs = P(("dp", "expert"), None)
    return jax.shard_map(body, mesh=mesh, in_specs=in_specs, out_specs=out_specs, check_vma=False)
```

time: 95.9 us -> 88.3 us (0.921)
  Pallas kernels: 92.8 us -> 86.6 us
  local copies, waits for them, and re-layouts: 2.84 us -> 1.53 us
    pallas_call x1, Pallas kernels: 92.8 us -> 86.6 us  [body(): pl.pallas_call(functools.partial(block_kernel, planes, columns), out_shap...]
    broadcast_in_dim x1 -> x0, local copies, waits for them, and re-layouts: 1.31 us -> none  [body(): norm_scale_vector[None]]
where the time goes in v3:
time: 88.3 us; the launch traced here: 88.1 us
  Pallas kernels  86.6 us (98%)
  local copies, waits for them, and re-layouts  1.53 us (2%)
    pallas_call x1, Pallas kernels, body(): pl.pallas_call(functools.partial(block_kernel, planes, columns), out_shap...  86.6 us

profile of v3, /device:TPU:1, one launch (start us, length us, event | category | flops | bytes accessed | tf_op | source)
XLA Modules:
  0.0 88.1 jit_solution(17387556045492598656)
XLA Ops:
  0.0 86.6 %shard_map.136 = bf16[12,2560]{1,0:T(8,128)(2,1)} custom-call(s32[12]{0:T(128)} %routes_ref.1, s32[12]{0:T(128)} %speaker_ref.1, s32[1,32]{1,0:T(1,128)} %slots_ref.1, bf16[12,2560]{1,0:T(8,128)(2,1)} %tokens_ref.1, f32[2560]{0:T(1024)} %gain_ref.1, bf16[16,2560]{1,0:T(8,128)(2,1)} %bitcast.7, bf16[1,2560,128]{2,1,0:T(8,128)(2,1)} %bitcast.4, ...), custom_call_target="tpu_custom_call" | custom-call | tf_op jit(solution)/shard_map/pallas_call | solution.py:581
  86.6 1.5 %copy.16 = bf16[12,2560]{1,0:T(8,128)(2,1)} copy(bf16[12,2560]{1,0:T(8,128)(2,1)} %shard_map.136) | data formatting | bytes 122880

commit v4 on v3

v4 whole, which is shorter than its diff:
```python
import functools

import jax
import jax.numpy as jnp
from jax import lax
from jax.experimental import pallas as pl
from jax.experimental.pallas import tpu as pltpu
from jax.sharding import PartitionSpec as P

MESH = pl.DeviceIdType.MESH
BF = jnp.bfloat16
F32 = jnp.float32
I32 = jnp.int32
norm_eps = 1e-05
ROWS = 16
REAL = 13
LANES = 128
PACK = 8


def iota(shape, dim):
    return lax.broadcasted_iota(I32, shape, dim)


def one_hot(condition):
    return jnp.where(condition, 1.0, 0.0).astype(BF)


def stack(rows, fill):
    tiles = rows.shape[1] // LANES
    columns = []
    for t in range(-(-tiles // PACK)):
        pieces = []
        for j in range(PACK):
            i = t * PACK + j
            if i < tiles:
                pieces.append(rows[:, i * LANES : (i + 1) * LANES])
            else:
                pieces.append(jnp.full((ROWS, LANES), fill if i == tiles else 0.0, rows.dtype))
        columns.append(jnp.concatenate(pieces, axis=0))
    return jnp.concatenate(columns, axis=1)


def tile_of(stacked, i):
    t, j = i // PACK, i % PACK
    return stacked[j * ROWS : (j + 1) * ROWS, t * LANES : (t + 1) * LANES]


def unstack(stacked, tiles):
    return jnp.concatenate([tile_of(stacked, i) for i in range(tiles)], axis=1)


def tight_tiles(tiles):
    return next(n for n in range(tiles) if (tiles - n) <= ROWS - REAL and REAL <= n)


def moving(n, axis):
    shape = (n * ROWS, (ROWS - REAL) * ROWS)
    a, b = iota(shape[::-1], 1) if axis else iota(shape, 0), iota(shape[::-1], 0) if axis else iota(shape, 1)
    return one_hot((a // ROWS == jnp.bitwise_and(b, ROWS - 1)) & (jnp.bitwise_and(a, ROWS - 1) == REAL + b // ROWS))


def overflow_of(block):
    below = jnp.concatenate([block[:, i * LANES : (i + 1) * LANES] for i in range(REAL)], axis=0)
    return dot(moving(REAL, 1), below).astype(BF)


def tighten(overflow, n):
    placed = dot(moving(n, 0), overflow)
    return jnp.concatenate([placed[i * ROWS : (i + 1) * ROWS] for i in range(n)], axis=1)


def dot(a, b):
    return jnp.dot(a, b, preferred_element_type=F32)


def dot_t(a, b):
    return lax.dot_general(a, b, (((0,), (0,)), ((), ())), preferred_element_type=F32)


def dot_nt(a, b):
    return lax.dot_general(a, b, (((1,), (1,)), ((), ())), preferred_element_type=F32)


def block_kernel(
    planes,
    columns,
    routes_in,
    speaker_in,
    slots_in,
    tokens_ref,
    gain_in,
    router_in,
    cg_ref,
    rg_ref,
    cu_ref,
    ru_ref,
    cd_ref,
    rd_ref,
    down_ref,
    up_ref,
    out_ref,
    routes_ref,
    speaker_ref,
    slots_ref,
    gain_ref,
    router_ref,
    in_sem,
    tok,
    w1,
    w2,
    wd,
    wu,
    xs,
    xr,
    ls,
    ls2,
    ls4,
    lr,
    rs,
    rr,
    bs,
    br,
    pack_ref,
    gath,
    hid,
    pb,
    first,
    rb,
    yb,
    own_sem,
    wsem,
    sent,
    got,
    exsem,
    ring_got,
    over_got,
    give_got,
):
    dp = lax.axis_index("dp")
    col = lax.axis_index("expert")
    z = dp // 2
    core = lax.rem(dp, 2)
    sessions, width = tokens_ref.shape
    tiles = width // LANES
    half = cg_ref.shape[2]
    hops = planes // 2
    tight = tight_tiles(tiles)
    left_out = tiles - tight
    cut = (tight + 1) // 2 * LANES
    sides = (pl.ds(0, cut), pl.ds(cut, tight * LANES - cut))
    sibling = (z * 2 + 1 - core, col)

    def plane(offset):
        return lax.rem(z + offset, planes)

    def remote(src, dst, send_sem, recv_sem, device):
        return pltpu.make_async_remote_copy(
            src, dst, send_sem, recv_sem, device_id=device, device_id_type=MESH
        )

    def group(view, index):
        return remote(view, view, sent.at[index], got.at[index], sibling)

    DISPATCH, RETURN, TO_ADAPTER, FROM_ADAPTER, GATHER, REDUCE, OVER, GIVE = 0, 2, 4, 5, 6, 7, 8, 9

    barrier = pltpu.get_barrier_semaphore()

    def greet(device):
        pl.semaphore_signal(barrier, inc=1, device_id=device, device_id_type=MESH)

    ring = 1
    while ring * ring < columns:
        ring += 1
    assert ring * ring == columns
    far_first = sorted(
        ((i, j) for i in range(ring) for j in range(ring)),
        key=lambda at: -sum(min(a, ring - a) for a in at),
    )

    def column(d):
        i, j = far_first[d]
        return lax.rem(col // ring + i, ring) * ring + lax.rem(lax.rem(col, ring) + j, ring)

    home = columns - 1
    near = ((plane(1) * 2 + core, col), (plane(planes - 1) * 2 + core, col))

    @pl.when(core == 1)
    def _():
        for device in near:
            greet(device)
        for d in range(home):
            greet((z * 2, column(d)))
            greet((z * 2 + 1, column(d)))
        greet(sibling)

    @pl.when(core == 0)
    def _():
        for d in range(1, planes):
            greet((plane(d) * 2, col))
        for d in range(columns):
            greet((z * 2 + 1, column(d)))

    fetched = (
        (routes_in, routes_ref),
        (speaker_in, speaker_ref),
        (slots_in, slots_ref),
        (gain_in, gain_ref),
        (router_in, router_ref),
    )
    fetches = [
        pltpu.make_async_copy(src, dst, in_sem.at[i]) for i, (src, dst) in enumerate(fetched)
    ]
    for copy in fetches:
        copy.start()
    for copy in fetches:
        copy.wait()

    tok[...] = jnp.zeros_like(tok)
    tok[0:sessions, :] = tokens_ref[...].astype(F32)
    x = tok[...]
    scale = lax.rsqrt(jnp.mean(x * x, axis=-1, keepdims=True) + norm_eps)
    normed = (x * scale * gain_ref[...][None, :]).astype(BF)

    routes = [routes_ref[s] for s in range(sessions)]
    route_slot = []
    for s in range(sessions):
        rank = jnp.int32(0)
        for earlier in range(s):
            rank = rank + jnp.where(routes[earlier] == routes[s], 1, 0)
        route_slot.append(routes[s] * 2 + rank)
    storage = [slots_ref[0, speaker_ref[s]] for s in range(sessions)]

    def spread(values, index):
        held = jnp.full(index.shape, -1, I32)
        for s in range(sessions):
            held = jnp.where(index == s, values[s], held)
        return held

    pairs = 2 * PACK
    outer = columns * pairs
    inner = PACK * ROWS
    row = iota((outer, inner), 0)
    lane = iota((outer, inner), 1)
    lane_session = jnp.bitwise_and(iota((1, inner), 1), ROWS - 1)
    same_piece = jnp.bitwise_and(row, PACK - 1) == lane // ROWS
    stacked = stack(normed, 1.0)
    to_expert = one_hot(same_piece & (row // PACK == spread(route_slot, lane_session)))
    xs[...] = dot(to_expert, stacked).astype(BF).reshape(xs.shape)
    def dispatch(d, source):
        return remote(
            xs.at[column(d)],
            xr.at[source, col],
            sent.at[DISPATCH + source],
            got.at[DISPATCH + source],
            (z * 2 + 1, column(d)),
        )

    def bring_back(d, h):
        return remote(
            rs.at[h, column(d)],
            rr.at[col],
            sent.at[RETURN + h],
            got.at[RETURN],
            (z * 2 + h, column(d)),
        )

    def over_planes(src, dst, index):
        for d in range(1, planes):
            to = plane(d)
            remote(src.at[to], dst.at[z], sent.at[index], got.at[index], (to * 2, col)).start()

    slots_copy = remote(ls, ls2, exsem.at[0, 0], exsem.at[1, 0], sibling)
    adapter_copies = (
        remote(down_ref.at[0, 0], wd.at[1], wsem.at[0, 6], wsem.at[1, 6], sibling),
        remote(up_ref.at[0, 0], wu.at[1], wsem.at[0, 7], wsem.at[1, 7], sibling),
    )

    @pl.when(core == 1)
    def _():
        pl.semaphore_wait(barrier, 2 * columns + 1)
        for d in range(home):
            dispatch(d, 1).start()
        xr[1, col] = xs[col]

    @pl.when(core == 0)
    def _():
        pl.semaphore_wait(barrier, columns + planes - 1)
        for d in range(columns):
            dispatch(d, 0).start()

    to_adapter = one_hot(same_piece & (row // PACK == spread(storage, lane_session)))
    tail = stacked[: inner // 2, 2 * LANES :]
    tail = jnp.concatenate([tail, tail], axis=0)
    tail = jnp.where(iota(tail.shape, 0) // (inner // 2) == core, tail.astype(F32), 0.0).astype(BF)
    stacked = jnp.concatenate([stacked[:, : 2 * LANES], tail], axis=1)
    ls[...] = dot(to_adapter, stacked).astype(BF).reshape(ls.shape)

    @pl.when(core == 1)
    def _():
        slots_copy.start()

    sources = (cg_ref, rg_ref, cu_ref, ru_ref)
    own = []
    for j in range(4):
        own.append(
            pltpu.make_async_copy(sources[j].at[0], w1.at[j, :, pl.ds(0, half)], own_sem.at[j])
        )
    for j, ref in enumerate((cd_ref, rd_ref)):
        own.append(
            pltpu.make_async_copy(ref.at[0], w2.at[pl.ds(2 * j * half, half)], own_sem.at[4 + j])
        )
    for copy in own:
        copy.start()
    adapter = (
        pltpu.make_async_copy(down_ref.at[0, 0], wd.at[0], own_sem.at[6]),
        pltpu.make_async_copy(up_ref.at[0, 0], wu.at[0], own_sem.at[7]),
    )

    @pl.when(core == 0)
    def _():
        for copy in adapter:
            copy.start()

    @pl.when(core == 0)
    def _():
        slots_copy.wait_recv()
        ls4[:, :, 0 : 2 * LANES] = ls[:, :, 0 : 2 * LANES]
        ls4[:, :, 2 * LANES : 4 * LANES] = ls2[:, :, 0 : 2 * LANES]
        ls4[:, :, 4 * LANES :] = ls[:, :, 2 * LANES :] + ls2[:, :, 2 * LANES :]
        over_planes(ls4, lr, TO_ADAPTER)
        lr[z] = ls4[z]

    shared = []
    for j in range(4):
        shared.append(
            remote(
                sources[j].at[0],
                w1.at[j, :, pl.ds(half, half)],
                wsem.at[0, j],
                wsem.at[1, j],
                sibling,
            )
        )
    for j, ref in enumerate((cd_ref, rd_ref)):
        shared.append(
            remote(
                ref.at[0],
                w2.at[pl.ds((2 * j + 1) * half, half)],
                wsem.at[0, 4 + j],
                wsem.at[1, 4 + j],
                sibling,
            )
        )
    for copy in shared:
        copy.start()

    @pl.when(core == 1)
    def _():
        for copy in adapter_copies:
            copy.start()

    wide_row = iota((inner, outer), 0)
    wide_lane = iota((inner, outer), 1)
    wide_piece = wide_row // ROWS == jnp.bitwise_and(wide_lane, PACK - 1)
    wide_index = jnp.bitwise_and(wide_row, ROWS - 1)

    def close_up(h):
        arrived = xr[h].reshape(outer, 3 * LANES)
        flags = jnp.where(
            jnp.bitwise_and(row, PACK - 1) == tiles % PACK, arrived[:, 2 * LANES :], 0.0
        ).astype(BF)
        left = iota((outer, outer), 0) // PACK
        right = iota((outer, outer), 1) // PACK
        before = dot_t(flags, one_hot(left < right))
        taken = dot_t(flags, one_hot(left == right))
        pack_ref[h] = one_hot(
            wide_piece & (taken > 0.5) & (jnp.abs(before - wide_index.astype(F32)) < 0.5)
        )
        placed = dot(pack_ref[h], arrived)
        over = jnp.concatenate([tile_of(placed, tight + i) for i in range(left_out)], axis=0)
        gath[z, pl.ds(h * ROWS, ROWS), :] = (
            unstack(placed, tight) + tighten(over.astype(BF), tight)
        ).astype(BF)

    def pick(half_index):
        return one_hot(
            wide_piece
            & (wide_index == wide_lane // pairs)
            & (jnp.bitwise_and(wide_lane // PACK, 1) == half_index)
        )

    def adapter_apply():
        group(lr.at[pl.ds(0, planes - 1)], TO_ADAPTER).wait()
        for copy in adapter:
            copy.wait()
        for copy in adapter_copies:
            copy.wait_recv()
        back = jnp.zeros((outer, 5 * LANES), F32)
        for r in range(2):
            chosen = pick(r)
            got = dot(chosen, lr[...].reshape(outer, 5 * LANES)).astype(BF)
            parts = []
            for source in range(2):
                pieces = []
                for i in range(tiles):
                    t, j = i // PACK, i % PACK
                    if t == 2:
                        t, j = 4, j + 4 * source
                    else:
                        t = t + 2 * source
                    pieces.append(got[j * ROWS : (j + 1) * ROWS, t * LANES : (t + 1) * LANES])
                parts.append(jnp.concatenate(pieces, axis=1))
            low = dot_nt(jnp.concatenate(parts, axis=0), wd[r]).astype(BF)
            delta = dot(low, wu[r]).astype(BF)
            first_stack, second_stack = stack(delta[:ROWS], 0.0), stack(delta[ROWS:], 0.0)
            both = jnp.concatenate(
                [first_stack[: inner // 2, 2 * LANES :], second_stack[: inner // 2, 2 * LANES :]],
                axis=0,
            )
            back += dot_t(
                chosen,
                jnp.concatenate(
                    [first_stack[:, : 2 * LANES], second_stack[:, : 2 * LANES], both], axis=1
                ),
            )
        bs[...] = back.astype(BF).reshape(bs.shape)
        over_planes(bs, br, FROM_ADAPTER)
        br[z] = bs[z]

    def length(d, part):
        return hops if part == d else hops - 1

    def from_plane(d, step):
        return plane(planes - step if d == 0 else step)

    def gather_copy(d, step, h, part):
        piece = gath.at[from_plane(d, step), pl.ds(h * ROWS, ROWS), sides[part]]
        return remote(piece, piece, sent.at[GATHER], ring_got.at[d, step, h, part], near[d])

    def hand_over(d, step):
        piece = gath.at[from_plane(d, step)]
        return remote(piece, piece, sent.at[OVER], over_got.at[d, step], sibling)

    reach = hops - 2
    middle = reach // 2
    inner_planes = [0]
    outer_planes = []
    for distance in range(1, reach + 1):
        both = [distance, planes - distance]
        if distance <= middle:
            inner_planes += both
        else:
            outer_planes = both + outer_planes
    given_planes = outer_planes + inner_planes[:0:-1] + [0]

    def weights_here():
        for copy in own:
            copy.wait()
        for copy in shared:
            copy.wait()

    def apply_experts(offsets):
        blocks = []
        for o in offsets:
            for h in range(2):
                block = gath[plane(o), pl.ds(h * ROWS, ROWS), :]
                over = overflow_of(block)
                blocks.append(
                    jnp.concatenate(
                        [block] + [over[i * ROWS : (i + 1) * ROWS] for i in range(left_out)], axis=1
                    )
                )
        rows = jnp.concatenate(blocks, axis=0)
        logits = dot_nt(rows, router_ref[...])
        chosen = jnp.where(iota(logits.shape, 1) == col, logits, 0.0)
        gate_prob = 1.0 / (1.0 + jnp.exp(-jnp.sum(chosen, axis=1, keepdims=True)))
        held = pl.ds(0, len(offsets) * 2 * ROWS)
        holds = jnp.bitwise_and(iota((len(offsets) * 2 * ROWS, 1), 0), ROWS - 1) < REAL
        for n in range(2):
            gate = dot(rows, w1[n])
            value = gate / (1.0 + jnp.exp(-gate)) * dot(rows, w1[2 + n])
            if n == 1:
                value = value * gate_prob
            value = jnp.where(holds, value, 0.0)
            hid[held, pl.ds(2 * n * half, 2 * half)] = value.astype(BF)

        over = dot(hid[held, :], w2[:, tight * LANES :]).astype(BF)
        for i, o in enumerate(offsets):
            for h in range(2):
                k = (i * 2 + h) * ROWS
                pieces = [
                    over[k : k + ROWS, j * LANES : (j + 1) * LANES] for j in range(left_out)
                ]
                pb[plane(o), pl.ds(h * ROWS, ROWS), :] = tighten(
                    jnp.concatenate(pieces, axis=0), tight
                ).astype(BF)

        def add_columns(cols):
            product = dot(hid[held, :], w2[:, cols])
            for i, o in enumerate(offsets):
                k = i * 2 * ROWS
                pb[plane(o), :, cols] = (
                    product[k : k + 2 * ROWS] + pb[plane(o), :, cols].astype(F32)
                ).astype(BF)

        @pl.loop(0, tight // 2)
        def _(t):
            add_columns(pl.ds(pl.multiple_of(t * 2 * LANES, 2 * LANES), 2 * LANES))

        if tight % 2:
            add_columns(pl.ds((tight - 1) * LANES, LANES))

    def give(offset):
        dest = plane(offset)
        return remote(pb.at[dest], pb.at[dest], sent.at[GIVE], give_got.at[offset], sibling)

    def reduce_copy(d, step, h, part):
        place = (pl.ds(h * ROWS, ROWS), sides[part])
        src = first.at[(d, *place)] if step == 0 else rb.at[(d, step - 1, *place)]
        return remote(
            src,
            rb.at[(d, step, *place)],
            sent.at[REDUCE],
            ring_got.at[d, step, h, part],
            near[d],
        )

    def reduce_step(step, chain, given):
        for h in (0, 1):
            for d in range(2):
                part = d if chain == hops else 1 - d
                place = (pl.ds(h * ROWS, ROWS), sides[part])
                offset = chain - step if d == 0 else planes - chain + step
                if offset in given_planes and offset not in given:
                    give(offset).wait_recv()
                    given.add(offset)
                dest = plane(offset)
                if step == 0:
                    first[(d, *place)] = pb[(dest, *place)]
                else:
                    reduce_copy(d, step - 1, h, part).wait_recv()
                    rb[(d, step - 1, *place)] = (
                        rb[(d, step - 1, *place)].astype(F32) + pb[(dest, *place)].astype(F32)
                    ).astype(BF)
                reduce_copy(d, step, h, part).start()

    @pl.when(core == 1)
    def _():
        for h in (1, 0):
            group(xr.at[h, pl.ds(0, columns - h)], DISPATCH + h).wait_recv()
            close_up(h)
            for part in range(2):
                for d in range(2):
                    gather_copy(d, 0, h, part).start()
        hand_over(0, 0).start()
        for step in range(1, hops + 1):
            if step == hops:
                weights_here()
                apply_experts([hops - 1, planes - hops + 1])
                reduce_step(0, hops - 1, set())
            for h in (1, 0):
                for part in range(2):
                    for d in range(2):
                        if step > length(d, part):
                            continue
                        gather_copy(d, step - 1, h, part).wait_recv()
                        if step < length(d, part):
                            gather_copy(d, step, h, part).start()
            if step <= reach:
                for d in range(2):
                    hand_over(d, step).start()
        apply_experts([hops])
        reduce_step(0, hops, set())

    @pl.when(core == 0)
    def _():
        weights_here()
        hand_over(0, 0).wait_recv()
        for step in range(1, reach + 1):
            for d in range(2):
                hand_over(d, step).wait_recv()
            if step == middle:
                apply_experts(inner_planes)
                adapter_apply()
        apply_experts(outer_planes)
        for offset in given_planes:
            give(offset).start()

    delta_copy = remote(br, br, exsem.at[0, 1], exsem.at[1, 1], sibling)

    @pl.when(core == 0)
    def _():
        group(br.at[pl.ds(0, planes - 1)], FROM_ADAPTER).wait()
        delta_copy.start()
        group(pb.at[pl.ds(0, len(given_planes))], GIVE).wait_send()
        delta_copy.wait_send()

    @pl.when(core == 1)
    def _():
        given = set()
        for step in range(1, hops):
            for chain in (hops - 1, hops):
                if step < chain:
                    reduce_step(step, chain, given)
        give(0).wait_recv()
        for h in (0, 1):
            for part in range(2):
                cols = sides[part]
                rows = pl.ds(h * ROWS, ROWS)
                value = pb[z, rows, cols].astype(F32)
                for d in range(2):
                    last = length(d, part) - 1
                    reduce_copy(d, last, h, part).wait_recv()
                    value = value + rb[d, last, rows, cols].astype(F32)
                yb[h, :, cols] = value.astype(BF)
            result = yb[h]
            pieces = [result[:, i * LANES : (i + 1) * LANES] for i in range(tight)]
            over = overflow_of(result)
            pieces += [over[i * ROWS : (i + 1) * ROWS] for i in range(left_out)]
            result = stack(jnp.concatenate(pieces, axis=1), 0.0)
            rs[h] = dot_t(pack_ref[h], result).astype(BF).reshape(rs.shape[1:])
            for d in range(home):
                bring_back(d, h).start()
            if h == 0:
                bring_back(home, h).start()
            else:
                rr[col] = rs[h, col]

    @pl.when(core == 1)
    def _():
        slots_copy.wait_send()
        for copy in adapter_copies:
            copy.wait_send()
        group(gath.at[pl.ds(0, planes - 1)], GATHER).wait_send()
        group(gath.at[pl.ds(0, planes - 1)], REDUCE).wait_send()
        group(gath.at[pl.ds(0, 2 * reach + 1)], OVER).wait_send()
        group(xs.at[pl.ds(0, columns - 1)], DISPATCH + 1).wait_send()
        delta_copy.wait_recv()

    @pl.when(core == 0)
    def _():
        group(xs, DISPATCH).wait_send()

    stored = spread(storage, wide_index) == wide_lane // PACK
    body_part = br[:, :, pl.ds(pl.multiple_of(core * 2 * LANES, 2 * LANES), 2 * LANES)]
    tail_part = br[:, :, 4 * LANES :].reshape(outer, LANES)
    tail_piece = wide_row // ROWS + 4 * core == jnp.bitwise_and(wide_lane, PACK - 1)
    total = jnp.concatenate(
        [
            dot(one_hot(wide_piece & stored), body_part.reshape(outer, 2 * LANES)),
            dot(one_hot(tail_piece & stored), tail_part),
        ],
        axis=1,
    )
    @pl.when(core == 1)
    def _():
        group(rr.at[pl.ds(0, columns - 1)], RETURN).wait_recv()
        group(rs.at[0], RETURN).wait_send()
        group(rs.at[1, pl.ds(0, columns - 1)], RETURN + 1).wait_send()

    @pl.when(core == 0)
    def _():
        group(rr, RETURN).wait_recv()

    from_expert = one_hot(wide_piece & (spread(route_slot, wide_index) == wide_lane // PACK))
    total += dot(from_expert, rr[...].reshape(outer, -1))
    for i in range(tiles):
        cols = pl.ds(i * LANES, LANES)
        out_ref[:, cols] = tile_of(total, i)[:sessions]


def body(
    tokens,
    norm_scale_vector,
    router,
    routes,
    session_speaker,
    adapter_slots,
    speaker_down_weight,
    speaker_up_weight,
    routed_gate_weight,
    routed_up_weight,
    routed_down_weight,
    common_gate_weight,
    common_up_weight,
    common_down_weight,
):
    sessions, width = tokens.shape
    planes = lax.axis_size("dp") // 2
    columns = lax.axis_size("expert")
    half = common_gate_weight.shape[1]
    rank = speaker_down_weight.shape[2]
    hops = planes // 2
    tight = tight_tiles(width // LANES) * LANES
    vmem = pl.BlockSpec(memory_space=pltpu.VMEM)
    hbm = pl.BlockSpec(memory_space=pl.ANY)
    dma = pltpu.SemaphoreType.DMA
    packed = pltpu.VMEM((columns, 2 * PACK, 3 * LANES), BF)
    packed_two = pltpu.VMEM((2, columns, 2 * PACK, 3 * LANES), BF)
    over_z = pltpu.VMEM((planes, 2 * PACK, 3 * LANES), BF)
    wide_z = pltpu.VMEM((planes, 2 * PACK, 5 * LANES), BF)
    total = pl.pallas_call(
        functools.partial(block_kernel, planes, columns),
        out_shape=jax.ShapeDtypeStruct((sessions, width), F32),
        in_specs=[hbm] * 3 + [vmem] + [hbm] * 10,
        out_specs=vmem,
        scratch_shapes=[
            pltpu.SMEM((sessions,), I32),
            pltpu.SMEM((sessions,), I32),
            pltpu.SMEM(adapter_slots.shape, I32),
            pltpu.VMEM((width,), F32),
            pltpu.VMEM((columns, width), BF),
            dma((5,)),
            pltpu.VMEM((ROWS, width), F32),
            pltpu.VMEM((4, width, 2 * half), BF),
            pltpu.VMEM((4 * half, width), BF),
            pltpu.VMEM((2, rank, width), BF),
            pltpu.VMEM((2, rank, width), BF),
            packed,
            packed_two,
            over_z,
            over_z,
            wide_z,
            wide_z,
            packed_two,
            packed,
            wide_z,
            wide_z,
            pltpu.VMEM((2, PACK * ROWS, columns * 2 * PACK), BF),
            pltpu.VMEM((planes, 2 * ROWS, tight), BF),
            pltpu.VMEM((planes * ROWS, 4 * half), BF),
            pltpu.VMEM((planes, 2 * ROWS, tight), BF),
            pltpu.VMEM((2, 2 * ROWS, tight), BF),
            pltpu.VMEM((2, hops, 2 * ROWS, tight), BF),
            pltpu.VMEM((2, ROWS, tight), BF),
            dma((8,)),
            dma((2, 8)),
            dma((10,)),
            dma((10,)),
            dma((2, 2)),
            dma((2, hops, 2, 2)),
            dma((2, hops - 1)),
            dma((planes,)),
        ],
        compiler_params=pltpu.CompilerParams(
            collective_id=1, has_side_effects=True, vmem_limit_bytes=56 * 1024 * 1024
        ),
    )(
        routes,
        session_speaker,
        adapter_slots,
        tokens,
        norm_scale_vector,
        router.T,
        common_gate_weight[None],
        routed_gate_weight,
        common_up_weight[None],
        routed_up_weight,
        common_down_weight[None],
        routed_down_weight,
        speaker_down_weight,
        speaker_up_weight,
    )
    return (tokens.astype(F32) + total).astype(BF)


def solution(mesh):
    in_specs = (
        P(("dp", "expert"), None),
        P(),
        P(),
        P(("dp", "expert")),
        P(("dp", "expert")),
        P("expert", None),
        P("expert", "dp", None, None),
        P("expert", "dp", None, None),
        P("expert", None, "dp"),
        P("expert", None, "dp"),
        P("expert", "dp", None),
        P(None, "dp"),
        P(None, "dp"),
        P("dp", None),
    )
    out_specs = P(("dp", "expert"), None)
    return jax.shard_map(body, mesh=mesh, in_specs=in_specs, out_specs=out_specs, check_vma=False)
```

time: 88.3 us -> 81.2 us (0.920)
  Pallas kernels: 86.6 us -> 79.3 us
  other arithmetic: 0 us -> 1.57 us
  local copies, waits for them, and re-layouts: 1.53 us -> 0.01 us
    pallas_call x1, Pallas kernels: 86.6 us -> 79.3 us  [body(): pl.pallas_call(functools.partial(block_kernel, planes, columns), out_shap...]
    convert_element_type x0 -> x1, other arithmetic: none -> 1.57 us  [body(): return (tokens.astype(F32) + total).astype(BF)]
    unnamed x1 -> x2, local copies, waits for them, and re-layouts: 1.53 us -> 0.01 us
where the time goes in v4:
time: 81.2 us; the launch traced here: 80.9 us
  Pallas kernels  79.3 us (98%)
  other arithmetic  1.57 us (2%)
    pallas_call x1, Pallas kernels, body(): pl.pallas_call(functools.partial(block_kernel, planes, columns), out_shap...  79.3 us

profile of v4, /device:TPU:1, one launch (start us, length us, event | category | flops | bytes accessed | tf_op | source)
XLA Modules:
  0.0 80.9 jit_solution(17222259247618186615)
XLA Ops:
  0.0 0.0 copy-start
  0.0 79.3 %shard_map.136 = f32[12,2560]{1,0:T(8,128)} custom-call(s32[12]{0:T(128)} %routes_in.1, s32[12]{0:T(128)} %speaker_in.1, s32[1,32]{1,0:T(1,128)} %slots_in.1, bf16[12,2560]{1,0:T(8,128)(2,1)} %tokens_ref.1, f32[2560]{0:T(1024)} %gain_in.1, bf16[16,2560]{1,0:T(8,128)(2,1)} %bitcast.7, bf16[1,2560,128]{2,1,0:T(8,128)(2,1)} %bitcast.4, ...), custom_call_target="tpu_custom_call" | custom-call | tf_op jit(solution)/shard_map/pallas_call | solution.py:703
  79.4 0.0 copy-done
  79.4 1.6 %add_convert_fusion = bf16[12,2560]{1,0:T(8,128)(2,1)} fusion(f32[12,2560]{1,0:T(8,128)} %shard_map.136, bf16[12,2560]{1,0:T(8,128)(2,1)S(1)} %copy-done), kind=kLoop, calls=%fused_computation | loop fusion | flops 92160 | bytes 245760 | tf_op jit(solution)/shard_map/convert_element_type | solution.py:765
Async XLA Ops:
  0.0 79.4 %copy-start = (bf16[12,2560]{1,0:T(8,128)(2,1)S(1)}, bf16[12,2560]{1,0:T(8,128)(2,1)}, u32[]{:S(2)}) copy-start(bf16[12,2560]{1,0:T(8,128)(2,1)} %tokens_ref.1) | copy-start | bytes 184324

commit v5 on v4

--- a/solution.py
+++ b/solution.py
@@ -12,6 +12,7 @@
 F32 = jnp.float32
 I32 = jnp.int32
 norm_eps = 1e-05
+PARTS = 2
 ROWS = 16
 REAL = 13
 LANES = 128
@@ -60,13 +61,13 @@
     return one_hot((a // ROWS == jnp.bitwise_and(b, ROWS - 1)) & (jnp.bitwise_and(a, ROWS - 1) == REAL + b // ROWS))
 
 
-def overflow_of(block):
+def overflow_of(block, out_of):
     below = jnp.concatenate([block[:, i * LANES : (i + 1) * LANES] for i in range(REAL)], axis=0)
-    return dot(moving(REAL, 1), below).astype(BF)
-
-
-def tighten(overflow, n):
-    placed = dot(moving(n, 0), overflow)
+    return dot(out_of[...], below).astype(BF)
+
+
+def tighten(overflow, n, into):
+    placed = dot(into[...], overflow)
     return jnp.concatenate([placed[i * ROWS : (i + 1) * ROWS] for i in range(n)], axis=1)
 
 
@@ -128,6 +129,9 @@
     first,
     rb,
     yb,
+    orders,
+    into,
+    out_of,
     own_sem,
     wsem,
     sent,
@@ -147,8 +151,8 @@
     hops = planes // 2
     tight = tight_tiles(tiles)
     left_out = tiles - tight
-    cut = (tight + 1) // 2 * LANES
-    sides = (pl.ds(0, cut), pl.ds(cut, tight * LANES - cut))
+    cuts = [-(-tight * i // PARTS) * LANES for i in range(PARTS + 1)]
+    sides = [pl.ds(a, b - a) for a, b in zip(cuts, cuts[1:])]
     sibling = (z * 2 + 1 - core, col)
 
     def plane(offset):
@@ -247,6 +251,13 @@
     stacked = stack(normed, 1.0)
     to_expert = one_hot(same_piece & (row // PACK == spread(route_slot, lane_session)))
     xs[...] = dot(to_expert, stacked).astype(BF).reshape(xs.shape)
+    to_adapter = one_hot(same_piece & (row // PACK == spread(storage, lane_session)))
+    tail = stacked[: inner // 2, 2 * LANES :]
+    tail = jnp.concatenate([tail, tail], axis=0)
+    tail = jnp.where(iota(tail.shape, 0) // (inner // 2) == core, tail.astype(F32), 0.0).astype(BF)
+    stacked = jnp.concatenate([stacked[:, : 2 * LANES], tail], axis=1)
+    ls[...] = dot(to_adapter, stacked).astype(BF).reshape(ls.shape)
+
     def dispatch(d, source):
         return remote(
             xs.at[column(d)],
@@ -266,19 +277,21 @@
         )
 
     def over_planes(src, dst, index):
-        for d in range(1, planes):
+        sign = -1 if index == TO_ADAPTER else 1
+        for d in sorted(range(1, planes), key=lambda d: sign * min(d, planes - d)):
             to = plane(d)
             remote(src.at[to], dst.at[z], sent.at[index], got.at[index], (to * 2, col)).start()
 
     slots_copy = remote(ls, ls2, exsem.at[0, 0], exsem.at[1, 0], sibling)
     adapter_copies = (
-        remote(down_ref.at[0, 0], wd.at[1], wsem.at[0, 6], wsem.at[1, 6], sibling),
-        remote(up_ref.at[0, 0], wu.at[1], wsem.at[0, 7], wsem.at[1, 7], sibling),
+        remote(down_ref.at[0, 0], wd.at[1], wsem.at[0, 2], wsem.at[1, 2], sibling),
+        remote(up_ref.at[0, 0], wu.at[1], wsem.at[0, 3], wsem.at[1, 3], sibling),
     )
 
     @pl.when(core == 1)
     def _():
         pl.semaphore_wait(barrier, 2 * columns + 1)
+        slots_copy.start()
         for d in range(home):
             dispatch(d, 1).start()
         xr[1, col] = xs[col]
@@ -288,39 +301,6 @@
         pl.semaphore_wait(barrier, columns + planes - 1)
         for d in range(columns):
             dispatch(d, 0).start()
-
-    to_adapter = one_hot(same_piece & (row // PACK == spread(storage, lane_session)))
-    tail = stacked[: inner // 2, 2 * LANES :]
-    tail = jnp.concatenate([tail, tail], axis=0)
-    tail = jnp.where(iota(tail.shape, 0) // (inner // 2) == core, tail.astype(F32), 0.0).astype(BF)
-    stacked = jnp.concatenate([stacked[:, : 2 * LANES], tail], axis=1)
-    ls[...] = dot(to_adapter, stacked).astype(BF).reshape(ls.shape)
-
-    @pl.when(core == 1)
-    def _():
-        slots_copy.start()
-
-    sources = (cg_ref, rg_ref, cu_ref, ru_ref)
-    own = []
-    for j in range(4):
-        own.append(
-            pltpu.make_async_copy(sources[j].at[0], w1.at[j, :, pl.ds(0, half)], own_sem.at[j])
-        )
-    for j, ref in enumerate((cd_ref, rd_ref)):
-        own.append(
-            pltpu.make_async_copy(ref.at[0], w2.at[pl.ds(2 * j * half, half)], own_sem.at[4 + j])
-        )
-    for copy in own:
-        copy.start()
-    adapter = (
-        pltpu.make_async_copy(down_ref.at[0, 0], wd.at[0], own_sem.at[6]),
-        pltpu.make_async_copy(up_ref.at[0, 0], wu.at[0], own_sem.at[7]),
-    )
-
-    @pl.when(core == 0)
-    def _():
-        for copy in adapter:
-            copy.start()
 
     @pl.when(core == 0)
     def _():
@@ -331,14 +311,36 @@
         over_planes(ls4, lr, TO_ADAPTER)
         lr[z] = ls4[z]
 
+    sources = (cg_ref, rg_ref, cu_ref, ru_ref)
+    own = []
+    for j in range(4):
+        own.append(
+            pltpu.make_async_copy(sources[j].at[0], w1.at[j, :, pl.ds(0, half)], own_sem.at[0])
+        )
+    for j, ref in enumerate((cd_ref, rd_ref)):
+        own.append(
+            pltpu.make_async_copy(ref.at[0], w2.at[pl.ds(2 * j * half, half)], own_sem.at[1])
+        )
+    for copy in own:
+        copy.start()
+    adapter = (
+        pltpu.make_async_copy(down_ref.at[0, 0], wd.at[0], own_sem.at[2]),
+        pltpu.make_async_copy(up_ref.at[0, 0], wu.at[0], own_sem.at[3]),
+    )
+
+    @pl.when(core == 0)
+    def _():
+        for copy in adapter:
+            copy.start()
+
     shared = []
     for j in range(4):
         shared.append(
             remote(
                 sources[j].at[0],
                 w1.at[j, :, pl.ds(half, half)],
-                wsem.at[0, j],
-                wsem.at[1, j],
+                wsem.at[0, 0],
+                wsem.at[1, 0],
                 sibling,
             )
         )
@@ -347,8 +349,8 @@
             remote(
                 ref.at[0],
                 w2.at[pl.ds((2 * j + 1) * half, half)],
-                wsem.at[0, 4 + j],
-                wsem.at[1, 4 + j],
+                wsem.at[0, 1],
+                wsem.at[1, 1],
                 sibling,
             )
         )
@@ -364,23 +366,28 @@
     wide_lane = iota((inner, outer), 1)
     wide_piece = wide_row // ROWS == jnp.bitwise_and(wide_lane, PACK - 1)
     wide_index = jnp.bitwise_and(wide_row, ROWS - 1)
+
+    slot_left = iota((outer, outer), 0) // PACK
+    slot_right = iota((outer, outer), 1) // PACK
+    orders[0] = one_hot(slot_left < slot_right)
+    orders[1] = one_hot(slot_left == slot_right)
+    into[...] = moving(tight, 0)
+    out_of[...] = moving(REAL, 1)
 
     def close_up(h):
         arrived = xr[h].reshape(outer, 3 * LANES)
         flags = jnp.where(
             jnp.bitwise_and(row, PACK - 1) == tiles % PACK, arrived[:, 2 * LANES :], 0.0
         ).astype(BF)
-        left = iota((outer, outer), 0) // PACK
-        right = iota((outer, outer), 1) // PACK
-        before = dot_t(flags, one_hot(left < right))
-        taken = dot_t(flags, one_hot(left == right))
+        before = dot_t(flags, orders[0])
+        taken = dot_t(flags, orders[1])
         pack_ref[h] = one_hot(
             wide_piece & (taken > 0.5) & (jnp.abs(before - wide_index.astype(F32)) < 0.5)
         )
         placed = dot(pack_ref[h], arrived)
         over = jnp.concatenate([tile_of(placed, tight + i) for i in range(left_out)], axis=0)
         gath[z, pl.ds(h * ROWS, ROWS), :] = (
-            unstack(placed, tight) + tighten(over.astype(BF), tight)
+            unstack(placed, tight) + tighten(over.astype(BF), tight, into)
         ).astype(BF)
 
     def pick(half_index):
@@ -428,20 +435,6 @@
         over_planes(bs, br, FROM_ADAPTER)
         br[z] = bs[z]
 
-    def length(d, part):
-        return hops if part == d else hops - 1
-
-    def from_plane(d, step):
-        return plane(planes - step if d == 0 else step)
-
-    def gather_copy(d, step, h, part):
-        piece = gath.at[from_plane(d, step), pl.ds(h * ROWS, ROWS), sides[part]]
-        return remote(piece, piece, sent.at[GATHER], ring_got.at[d, step, h, part], near[d])
-
-    def hand_over(d, step):
-        piece = gath.at[from_plane(d, step)]
-        return remote(piece, piece, sent.at[OVER], over_got.at[d, step], sibling)
-
     reach = hops - 2
     middle = reach // 2
     inner_planes = [0]
@@ -454,18 +447,34 @@
             outer_planes = both + outer_planes
     given_planes = outer_planes + inner_planes[:0:-1] + [0]
 
+    def length(d, part):
+        return hops if part // (PARTS // 2) == d else hops - 1
+
+    def from_plane(d, step):
+        return plane(planes - step if d == 0 else step)
+
+    def gather_copy(d, step, h, part):
+        piece = gath.at[from_plane(d, step), pl.ds(h * ROWS, ROWS), sides[part]]
+        return remote(piece, piece, sent.at[GATHER], ring_got.at[d, step, h, part], near[d])
+
+    def hand_over(d, step):
+        piece = gath.at[from_plane(d, step)]
+        batch = 0 if step <= middle else 1
+        return remote(piece, piece, sent.at[OVER], over_got.at[batch], sibling)
+
     def weights_here():
-        for copy in own:
-            copy.wait()
-        for copy in shared:
-            copy.wait()
+        gate_up, down = w1.at[:, :, pl.ds(0, half)], w2.at[pl.ds(0, 2 * half)]
+        pltpu.make_async_copy(gate_up, gate_up, own_sem.at[0]).wait()
+        pltpu.make_async_copy(down, down, own_sem.at[1]).wait()
+        remote(gate_up, gate_up, wsem.at[0, 0], wsem.at[1, 0], sibling).wait()
+        remote(down, down, wsem.at[0, 1], wsem.at[1, 1], sibling).wait()
 
     def apply_experts(offsets):
         blocks = []
         for o in offsets:
             for h in range(2):
                 block = gath[plane(o), pl.ds(h * ROWS, ROWS), :]
-                over = overflow_of(block)
+                over = overflow_of(block, out_of)
                 blocks.append(
                     jnp.concatenate(
                         [block] + [over[i * ROWS : (i + 1) * ROWS] for i in range(left_out)], axis=1
@@ -493,7 +502,7 @@
                     over[k : k + ROWS, j * LANES : (j + 1) * LANES] for j in range(left_out)
                 ]
                 pb[plane(o), pl.ds(h * ROWS, ROWS), :] = tighten(
-                    jnp.concatenate(pieces, axis=0), tight
+                    jnp.concatenate(pieces, axis=0), tight, into
                 ).astype(BF)
 
         def add_columns(cols):
@@ -513,7 +522,11 @@
 
     def give(offset):
         dest = plane(offset)
-        return remote(pb.at[dest], pb.at[dest], sent.at[GIVE], give_got.at[offset], sibling)
+        return remote(pb.at[dest], pb.at[dest], sent.at[GIVE], give_got.at[0 if offset in outer_planes else 1], sibling)
+
+    def given_here(kind, batch):
+        view = pb.at[pl.ds(0, len(kind))]
+        remote(view, view, sent.at[GIVE], give_got.at[batch], sibling).wait_recv()
 
     def reduce_copy(d, step, h, part):
         place = (pl.ds(h * ROWS, ROWS), sides[part])
@@ -528,29 +541,34 @@
 
     def reduce_step(step, chain, given):
         for h in (0, 1):
-            for d in range(2):
-                part = d if chain == hops else 1 - d
-                place = (pl.ds(h * ROWS, ROWS), sides[part])
-                offset = chain - step if d == 0 else planes - chain + step
-                if offset in given_planes and offset not in given:
-                    give(offset).wait_recv()
-                    given.add(offset)
-                dest = plane(offset)
-                if step == 0:
-                    first[(d, *place)] = pb[(dest, *place)]
-                else:
-                    reduce_copy(d, step - 1, h, part).wait_recv()
-                    rb[(d, step - 1, *place)] = (
-                        rb[(d, step - 1, *place)].astype(F32) + pb[(dest, *place)].astype(F32)
-                    ).astype(BF)
-                reduce_copy(d, step, h, part).start()
+            for part in range(PARTS):
+                for d in range(2):
+                    if length(d, part) == chain:
+                        reduce_piece(step, chain, given, h, part, d)
+
+    def reduce_piece(step, chain, given, h, part, d):
+        place = (pl.ds(h * ROWS, ROWS), sides[part])
+        offset = chain - step if d == 0 else planes - chain + step
+        for batch, kind in enumerate((outer_planes, inner_planes)):
+            if offset in kind and batch not in given:
+                given_here(kind, batch)
+                given.add(batch)
+        dest = plane(offset)
+        if step == 0:
+            first[(d, *place)] = pb[(dest, *place)]
+        else:
+            reduce_copy(d, step - 1, h, part).wait_recv()
+            rb[(d, step - 1, *place)] = (
+                rb[(d, step - 1, *place)].astype(F32) + pb[(dest, *place)].astype(F32)
+            ).astype(BF)
+        reduce_copy(d, step, h, part).start()
 
     @pl.when(core == 1)
     def _():
         for h in (1, 0):
             group(xr.at[h, pl.ds(0, columns - h)], DISPATCH + h).wait_recv()
             close_up(h)
-            for part in range(2):
+            for part in range(PARTS):
                 for d in range(2):
                     gather_copy(d, 0, h, part).start()
         hand_over(0, 0).start()
@@ -560,7 +578,7 @@
                 apply_experts([hops - 1, planes - hops + 1])
                 reduce_step(0, hops - 1, set())
             for h in (1, 0):
-                for part in range(2):
+                for part in range(PARTS):
                     for d in range(2):
                         if step > length(d, part):
                             continue
@@ -576,13 +594,12 @@
     @pl.when(core == 0)
     def _():
         weights_here()
-        hand_over(0, 0).wait_recv()
-        for step in range(1, reach + 1):
-            for d in range(2):
-                hand_over(d, step).wait_recv()
-            if step == middle:
-                apply_experts(inner_planes)
-                adapter_apply()
+        inner_view = gath.at[pl.ds(0, len(inner_planes))]
+        remote(inner_view, inner_view, sent.at[OVER], over_got.at[0], sibling).wait_recv()
+        apply_experts(inner_planes)
+        adapter_apply()
+        outer_view = gath.at[pl.ds(0, len(outer_planes))]
+        remote(outer_view, outer_view, sent.at[OVER], over_got.at[1], sibling).wait_recv()
         apply_experts(outer_planes)
         for offset in given_planes:
             give(offset).start()
@@ -603,9 +620,8 @@
             for chain in (hops - 1, hops):
                 if step < chain:
                     reduce_step(step, chain, given)
-        give(0).wait_recv()
         for h in (0, 1):
-            for part in range(2):
+            for part in range(PARTS):
                 cols = sides[part]
                 rows = pl.ds(h * ROWS, ROWS)
                 value = pb[z, rows, cols].astype(F32)
@@ -616,7 +632,7 @@
                 yb[h, :, cols] = value.astype(BF)
             result = yb[h]
             pieces = [result[:, i * LANES : (i + 1) * LANES] for i in range(tight)]
-            over = overflow_of(result)
+            over = overflow_of(result, out_of)
             pieces += [over[i * ROWS : (i + 1) * ROWS] for i in range(left_out)]
             result = stack(jnp.concatenate(pieces, axis=1), 0.0)
             rs[h] = dot_t(pack_ref[h], result).astype(BF).reshape(rs.shape[1:])
@@ -734,14 +750,17 @@
             pltpu.VMEM((2, 2 * ROWS, tight), BF),
             pltpu.VMEM((2, hops, 2 * ROWS, tight), BF),
             pltpu.VMEM((2, ROWS, tight), BF),
-            dma((8,)),
-            dma((2, 8)),
+            pltpu.VMEM((2, columns * 2 * PACK, columns * 2 * PACK), BF),
+            pltpu.VMEM((tight // LANES * ROWS, (ROWS - REAL) * ROWS), BF),
+            pltpu.VMEM(((ROWS - REAL) * ROWS, REAL * ROWS), BF),
+            dma((4,)),
+            dma((2, 4)),
             dma((10,)),
             dma((10,)),
             dma((2, 2)),
-            dma((2, hops, 2, 2)),
-            dma((2, hops - 1)),
-            dma((planes,)),
+            dma((2, hops, 2, PARTS)),
+            dma((2,)),
+            dma((2,)),
         ],
         compiler_params=pltpu.CompilerParams(
             collective_id=1, has_side_effects=True, vmem_limit_bytes=56 * 1024 * 1024

time: 81.2 us -> 79.7 us (0.982)
  Pallas kernels: 79.3 us -> 77.9 us
    pallas_call x1, Pallas kernels: 79.3 us -> 77.9 us  [body(): pl.pallas_call(functools.partial(block_kernel, planes, columns), out_shap...]
where the time goes in v5:
time: 79.7 us; the launch traced here: 79.5 us
  Pallas kernels  77.9 us (98%)
  other arithmetic  1.57 us (2%)
    pallas_call x1, Pallas kernels, body(): pl.pallas_call(functools.partial(block_kernel, planes, columns), out_shap...  77.9 us

profile of v5, /device:TPU:1, one launch (start us, length us, event | category | flops | bytes accessed | tf_op | source)
XLA Modules:
  0.0 79.5 jit_solution(6786753178303830774)
XLA Ops:
  0.0 0.0 copy-start
  0.0 77.9 %shard_map.136 = f32[12,2560]{1,0:T(8,128)} custom-call(s32[12]{0:T(128)} %routes_in.1, s32[12]{0:T(128)} %speaker_in.1, s32[1,32]{1,0:T(1,128)} %slots_in.1, bf16[12,2560]{1,0:T(8,128)(2,1)} %tokens_ref.1, f32[2560]{0:T(1024)} %gain_in.1, bf16[16,2560]{1,0:T(8,128)(2,1)} %bitcast.7, bf16[1,2560,128]{2,1,0:T(8,128)(2,1)} %bitcast.4, ...), custom_call_target="tpu_custom_call" | custom-call | tf_op jit(solution)/shard_map/pallas_call | solution.py:719
  77.9 0.0 copy-done
  77.9 1.6 %add_convert_fusion = bf16[12,2560]{1,0:T(8,128)(2,1)} fusion(f32[12,2560]{1,0:T(8,128)} %shard_map.136, bf16[12,2560]{1,0:T(8,128)(2,1)S(1)} %copy-done), kind=kLoop, calls=%fused_computation | loop fusion | flops 92160 | bytes 245760 | tf_op jit(solution)/shard_map/convert_element_type | solution.py:784
Async XLA Ops:
  0.0 77.9 %copy-start = (bf16[12,2560]{1,0:T(8,128)(2,1)S(1)}, bf16[12,2560]{1,0:T(8,128)(2,1)}, u32[]{:S(2)}) copy-start(bf16[12,2560]{1,0:T(8,128)(2,1)} %tokens_ref.1) | copy-start | bytes 184324

commit v6 on v5

--- a/solution.py
+++ b/solution.py
@@ -188,10 +188,11 @@
 
     home = columns - 1
     near = ((plane(1) * 2 + core, col), (plane(planes - 1) * 2 + core, col))
+    next_but_one = ((plane(2) * 2 + core, col), (plane(planes - 2) * 2 + core, col))
 
     @pl.when(core == 1)
     def _():
-        for device in near:
+        for device in near + next_but_one:
             greet(device)
         for d in range(home):
             greet((z * 2, column(d)))
@@ -290,7 +291,7 @@
 
     @pl.when(core == 1)
     def _():
-        pl.semaphore_wait(barrier, 2 * columns + 1)
+        pl.semaphore_wait(barrier, 2 * columns + 3)
         slots_copy.start()
         for d in range(home):
             dispatch(d, 1).start()
@@ -457,6 +458,11 @@
         piece = gath.at[from_plane(d, step), pl.ds(h * ROWS, ROWS), sides[part]]
         return remote(piece, piece, sent.at[GATHER], ring_got.at[d, step, h, part], near[d])
 
+    def gather_skip(d, h, part):
+        piece = gath.at[from_plane(d, hops - 2), pl.ds(h * ROWS, ROWS), sides[part]]
+        got_at = ring_got.at[d, hops - 1, h, part]
+        return remote(piece, piece, sent.at[GATHER], got_at, next_but_one[d])
+
     def hand_over(d, step):
         piece = gath.at[from_plane(d, step)]
         batch = 0 if step <= middle else 1
@@ -530,13 +536,21 @@
 
     def reduce_copy(d, step, h, part):
         place = (pl.ds(h * ROWS, ROWS), sides[part])
-        src = first.at[(d, *place)] if step == 0 else rb.at[(d, step - 1, *place)]
+        device = near[d]
+        if step == 0:
+            src = first.at[(d, *place)]
+            if length(d, part) == hops:
+                device = next_but_one[d]
+        elif step == 1 and length(d, part) == hops:
+            src = pb.at[(plane(hops - 1 if d == 0 else planes - hops + 1), *place)]
+        else:
+            src = rb.at[(d, step - 1, *place)]
         return remote(
             src,
             rb.at[(d, step, *place)],
             sent.at[REDUCE],
             ring_got.at[d, step, h, part],
-            near[d],
+            device,
         )
 
     def reduce_step(step, chain, given):
@@ -556,11 +570,13 @@
         dest = plane(offset)
         if step == 0:
             first[(d, *place)] = pb[(dest, *place)]
-        else:
+        elif step > 1 or chain < hops:
+            value = pb[(dest, *place)].astype(F32)
+            if step == 2 and chain == hops:
+                reduce_copy(d, 0, h, part).wait_recv()
+                value = value + rb[(d, 0, *place)].astype(F32)
             reduce_copy(d, step - 1, h, part).wait_recv()
-            rb[(d, step - 1, *place)] = (
-                rb[(d, step - 1, *place)].astype(F32) + pb[(dest, *place)].astype(F32)
-            ).astype(BF)
+            rb[(d, step - 1, *place)] = (rb[(d, step - 1, *place)].astype(F32) + value).astype(BF)
         reduce_copy(d, step, h, part).start()
 
     @pl.when(core == 1)
@@ -577,14 +593,17 @@
                 weights_here()
                 apply_experts([hops - 1, planes - hops + 1])
                 reduce_step(0, hops - 1, set())
+                reduce_step(1, hops, set())
             for h in (1, 0):
                 for part in range(PARTS):
                     for d in range(2):
                         if step > length(d, part):
                             continue
                         gather_copy(d, step - 1, h, part).wait_recv()
-                        if step < length(d, part):
+                        if step < hops - 1:
                             gather_copy(d, step, h, part).start()
+                        if step == hops - 2 and length(d, part) == hops:
+                            gather_skip(d, h, part).start()
             if step <= reach:
                 for d in range(2):
                     hand_over(d, step).start()
@@ -618,7 +637,7 @@
         given = set()
         for step in range(1, hops):
             for chain in (hops - 1, hops):
-                if step < chain:
+                if step < chain and (step, chain) != (1, hops):
                     reduce_step(step, chain, given)
         for h in (0, 1):
             for part in range(PARTS):
@@ -683,7 +702,7 @@
     total += dot(from_expert, rr[...].reshape(outer, -1))
     for i in range(tiles):
         cols = pl.ds(i * LANES, LANES)
-        out_ref[:, cols] = tile_of(total, i)[:sessions]
+        out_ref[:, cols] = (tok[:, cols] + tile_of(total, i))[:sessions].astype(BF)
 
 
 def body(
@@ -716,9 +735,9 @@
     packed_two = pltpu.VMEM((2, columns, 2 * PACK, 3 * LANES), BF)
     over_z = pltpu.VMEM((planes, 2 * PACK, 3 * LANES), BF)
     wide_z = pltpu.VMEM((planes, 2 * PACK, 5 * LANES), BF)
-    total = pl.pallas_call(
+    return pl.pallas_call(
         functools.partial(block_kernel, planes, columns),
-        out_shape=jax.ShapeDtypeStruct((sessions, width), F32),
+        out_shape=jax.ShapeDtypeStruct((sessions, width), BF),
         in_specs=[hbm] * 3 + [vmem] + [hbm] * 10,
         out_specs=vmem,
         scratch_shapes=[
@@ -781,7 +800,6 @@
         speaker_down_weight,
         speaker_up_weight,
     )
-    return (tokens.astype(F32) + total).astype(BF)
 
 
 def solution(mesh):

time: 79.7 us -> 79.6 us (level)
  other arithmetic: 1.57 us -> 0 us
  local copies, waits for them, and re-layouts: 0.01 us -> 1.53 us
    convert_element_type x1 -> x0, other arithmetic: 1.57 us -> none  [body(): return (tokens.astype(F32) + total).astype(BF)]
    unnamed x2 -> x1, local copies, waits for them, and re-layouts: 0.01 us -> 1.53 us
where the time goes in v6:
time: 79.6 us; the launch traced here: 79.4 us
  Pallas kernels  77.9 us (98%)
  local copies, waits for them, and re-layouts  1.53 us (2%)
    pallas_call x1, Pallas kernels, body(): pl.pallas_call(functools.partial(block_kernel, planes, columns), out_shap...  77.9 us

profile of v6, /device:TPU:1, one launch (start us, length us, event | category | flops | bytes accessed | tf_op | source)
XLA Modules:
  0.0 79.4 jit_solution(1912062278801865767)
XLA Ops:
  0.0 77.9 %shard_map.136 = bf16[12,2560]{1,0:T(8,128)(2,1)} custom-call(s32[12]{0:T(128)} %routes_in.1, s32[12]{0:T(128)} %speaker_in.1, s32[1,32]{1,0:T(1,128)} %slots_in.1, bf16[12,2560]{1,0:T(8,128)(2,1)} %tokens_ref.1, f32[2560]{0:T(1024)} %gain_in.1, bf16[16,2560]{1,0:T(8,128)(2,1)} %bitcast.7, bf16[1,2560,128]{2,1,0:T(8,128)(2,1)} %bitcast.4, ...), custom_call_target="tpu_custom_call" | custom-call | tf_op jit(solution)/shard_map/pallas_call | solution.py:738
  77.9 1.5 %copy.16 = bf16[12,2560]{1,0:T(8,128)(2,1)} copy(bf16[12,2560]{1,0:T(8,128)(2,1)} %shard_map.136) | data formatting | bytes 122880
